TPU v7x, 256 devices: a whole 4x4x8 slice. The times are simulated.
256 devices in a mesh: row: 16 (over z, y_hi), col: 16 (over x, y_lo, core).
Axes of the slice: x: 4, y: 4 (y_hi: 2, y_lo: 2; y = y_hi * 2 + y_lo), z: 8, core: 2. Of those that a mesh axis runs over, the one named last changes fastest.
Arguments:
- orbitals: bfloat16 [256, 64000], P(('row', 'col')), may hold values from -6 to 6
- pair_list: int32 [256, 8, 2], P(('row', 'col')), may hold values from 0 to 15, as said below
- pair_count: int32 [256], P(('row', 'col')), may hold values from 1 to 8
Outputs:
- exchange_fields: float32 [256, 64000], P(('row', 'col'))
Inputs may be any that keep to these rules, and one draw needn't show every extreme that they name: pair_list[., ., 0] is below 16 and pair_list[., ., 1] below 16.
All inputs are finite; a program needn't handle non-finite values.
Results may differ from a plain program's by a relative error of at most 0.0004.
Values may be sent and summed in bfloat16 or wider, within the bound.
A program may use at most 64 MiB of HBM per device.

v0:
```python
import jax
import jax.numpy as jnp
from jax import lax
from jax.sharding import PartitionSpec as P

GX = 40


screen_width = 0.9
axis_forms = ("kx,xyz->kyz", "ky,xyz->xkz", "kz,xyz->xyk")


def contract(pattern, operator, values):
    return jnp.einsum(
        pattern,
        operator,
        values,
        precision=lax.Precision.HIGHEST,
        preferred_element_type=jnp.float32,
    )


def dft_tables(length):
    counter = lax.iota(jnp.int32, length)
    phases = (counter[:, None] * counter[None, :] % length).astype(jnp.float32) * (
        2.0 * jnp.pi / length
    )
    frequency = jnp.where(counter < length // 2, counter, counter - length).astype(jnp.float32) * (
        2.0 * jnp.pi / length
    )
    squared = frequency * frequency
    squared_sum = squared[:, None, None] + squared[None, :, None] + squared[None, None, :]
    safe_sum = jnp.where(squared_sum > 0, squared_sum, 1.0)
    screened = 4.0 * jnp.pi * (1.0 - jnp.exp(-safe_sum / (4.0 * screen_width**2))) / safe_sum
    kernel = jnp.where(squared_sum > 0, screened, jnp.pi / screen_width**2)
    return (jnp.cos(phases), jnp.sin(phases), kernel)


def solve_potential(density, cosine_table, sine_table, kernel):
    length = density.shape[0]
    real_part = contract(axis_forms[0], cosine_table, density)
    imag_part = -contract(axis_forms[0], sine_table, density)
    for pattern in axis_forms[1:]:
        real_part, imag_part = (
            contract(pattern, cosine_table, real_part) + contract(pattern, sine_table, imag_part),
            contract(pattern, cosine_table, imag_part) - contract(pattern, sine_table, real_part),
        )
    real_part = real_part * kernel
    imag_part = imag_part * kernel
    for pattern in axis_forms[:2]:
        real_part, imag_part = (
            contract(pattern, cosine_table, real_part) - contract(pattern, sine_table, imag_part),
            contract(pattern, sine_table, real_part) + contract(pattern, cosine_table, imag_part),
        )
    real_part = contract(axis_forms[2], cosine_table, real_part) - contract(
        axis_forms[2], sine_table, imag_part
    )
    return real_part / float(length**3)


def set_row(terms_block, slot, values):
    return lax.dynamic_update_index_in_dim(terms_block, values[None, :], slot, 0)


def collect_rows(band_rows, terms_block, count):
    wanted = lax.iota(jnp.int32, count)
    selector = (wanted[:, None] == band_rows[None, :]).astype(jnp.float32)
    return jnp.dot(
        selector, terms_block, precision=lax.Precision.HIGHEST, preferred_element_type=jnp.float32
    )


def shards(orbitals, pair_list, pair_count):
    per_device = orbitals.shape[0]
    grid_size = orbitals.shape[1]
    column_count = lax.axis_size("col")
    row_index = lax.axis_index("row")
    col_index = lax.axis_index("col")
    first_local = pair_list[0, :, 0]
    second_local = pair_list[0, :, 1]
    pair_total = pair_count[0]
    slot_count = pair_list.shape[1]
    first_global = row_index * (per_device * column_count) + first_local
    second_global = (
        second_local // per_device * column_count + col_index
    ) * per_device + second_local % per_device
    distinct = jnp.where(first_global != second_global, 1.0, 0.0).astype(jnp.float32)
    cosine_table, sine_table, kernel = dft_tables(GX)
    column_block = lax.all_gather(orbitals, "row", axis=0, tiled=True)
    empty_terms = jnp.zeros((slot_count, grid_size), jnp.float32)

    def pair_terms(terms, pair_slot, first_wave):
        first_terms, second_terms = terms
        second_row = second_local[pair_slot]
        second_wave = lax.dynamic_index_in_dim(column_block, second_row, 0, keepdims=False).astype(
            jnp.float32
        )
        density = (first_wave * second_wave).reshape(GX, GX, GX)
        potential = solve_potential(density, cosine_table, sine_table, kernel).reshape(-1)
        first_terms = set_row(first_terms, pair_slot, potential * second_wave)
        second_terms = set_row(
            second_terms, pair_slot, distinct[pair_slot] * potential * first_wave
        )
        return (first_terms, second_terms)

    row_block = lax.all_gather(orbitals, "col", axis=0, tiled=True)

    def visit_pair(pair_slot, terms):
        first_row = first_local[pair_slot]
        first_wave = lax.dynamic_index_in_dim(row_block, first_row, 0, keepdims=False).astype(
            jnp.float32
        )
        return pair_terms(terms, pair_slot, first_wave)

    first_terms, second_terms = lax.fori_loop(0, pair_total, visit_pair, (empty_terms, empty_terms))
    first_rows_total = per_device * column_count
    second_rows_total = column_block.shape[0]
    first_fields = collect_rows(first_local, first_terms, first_rows_total)
    second_fields = collect_rows(second_local, second_terms, second_rows_total)
    own_first = lax.psum_scatter(first_fields, "col", scatter_dimension=0, tiled=True)
    own_second = lax.psum_scatter(second_fields, "row", scatter_dimension=0, tiled=True)
    return own_first + own_second


def solution(mesh):
    return jax.shard_map(
        shards,
        mesh=mesh,
        in_specs=(P(("row", "col"), None), P(("row", "col"), None, None), P(("row", "col"))),
        out_specs=P(("row", "col"), None),
        check_vma=False,
    )
```

profile of v0, /device:TPU:8, one launch (start us, length us, event | category | flops | bytes accessed | tf_op | source)
XLA Modules:
  0.0 906.3 jit_solution(3824748803942726698)
XLA Ops:
  9.7 41.9 %all-gather.5.cloned.1.call-done = bf16[16,1,64000]{2,1,0:T(2,128)(2,1)} async-done(((bf16[1,1,64000]{2,1,0:T(2,128)(2,1)}), bf16[16,1,64000]{2,1,0:T(2,128)(2,1)}) %all-gather.5.cloned.1.call-update) | async-done | bytes 2048016 | tf_op jit(solution)/shard_map/all_gather | solution.py:106
  51.6 2.4 copy.63
  54.0 99.3 %all-gather.7.cloned.1.call-done = bf16[16,1,64000]{2,1,0:T(2,128)(2,1)} async-done(((bf16[1,1,64000]{2,1,0:T(2,128)(2,1)}), bf16[16,1,64000]{2,1,0:T(2,128)(2,1)}) %all-gather.7.cloned.1.call-update) | async-done | bytes 2048016 | tf_op jit(solution)/shard_map/all_gather | solution.py:89
  153.3 3.7 copy.62
  159.9 340.1 %while.14 = (s32[]{:T(128)}, f32[8,64000]{1,0:T(8,128)}, f32[8,64000]{1,0:T(8,128)}, s32[]{:T(128)}, s32[8]{0:T(128)S(1)}, /*index=5*/bf16[16,64000]{1,0:T(8,128...) while((s32[]{:T(128)}, f32[8,64000]{1,0:T(8,128)}, ...), condition=%wide.region_1.2_spmd.clone.clone, body=%wide.region_0.1_spmd.clone.clone.sunk | while | flops 617184000 | bytes 36109480 | solution.py:115
  165.7 2.2 multiply_reduce_fusion.2
  194.0 2.5 multiply_multiply_fusion.2
  196.5 6.0 dynamic_update_slice.14
  202.4 6.0 dynamic_update_slice.13
  242.4 2.5 multiply_multiply_fusion.2
  244.9 6.0 dynamic_update_slice.14
  250.9 6.0 dynamic_update_slice.13
  290.9 2.5 multiply_multiply_fusion.2
  293.4 6.0 dynamic_update_slice.14
  299.4 6.0 dynamic_update_slice.13
  339.4 2.5 multiply_multiply_fusion.2
  341.8 6.0 dynamic_update_slice.14
  347.8 6.0 dynamic_update_slice.13
  387.8 2.5 multiply_multiply_fusion.2
  390.3 6.0 dynamic_update_slice.14
  396.3 6.0 dynamic_update_slice.13
  436.3 2.5 multiply_multiply_fusion.2
  438.8 6.0 dynamic_update_slice.14
  444.8 6.0 dynamic_update_slice.13
  484.8 2.5 multiply_multiply_fusion.2
  487.2 6.0 dynamic_update_slice.14
  493.2 6.0 dynamic_update_slice.13
  500.0 5.2 fusion.199
  506.8 3.7 fusion.200
  512.4 168.7 %all-reduce.5.cloned.1.call-done = f32[16,64000]{1,0:T(8,128)} async-done(((f32[16,64000]{1,0:T(8,128)}), f32[16,64000]{1,0:T(8,128)}) %all-reduce.5.cloned.1.call-update) | async-done | bytes 4096016
  681.1 214.2 %all-reduce.7.cloned.1.call-done = f32[16,64000]{1,0:T(8,128)} async-done(((f32[16,64000]{1,0:T(8,128)}), f32[16,64000]{1,0:T(8,128)}) %all-reduce.7.cloned.1.call-update) | async-done | bytes 4096016
  895.3 4.5 dynamic-slice_add_fusion
  (280 shorter events, 212.6 us)
Async XLA Ops:
  6.5 45.1 %all-gather.5.cloned.1.call-start = ((), (), s32[]{:S(2)}) async-start(), calls=%async_computation | async-start | bytes 4352000 | tf_op jit(solution)/shard_map/all_gather | solution.py:106
  7.3 146.1 %all-gather.7.cloned.1.call-start = ((), (), s32[]{:S(2)}) async-start(), calls=%async_computation.1 | async-start | bytes 4352000 | tf_op jit(solution)/shard_map/all_gather | solution.py:89
  8.0 673.1 %all-reduce.5.cloned.1.call-start = ((), (), s32[]{:S(2)}) async-start(), calls=%async_computation.2 | async-start | bytes 8192000
  160.6 7.4 copy-start
  191.1 2.8 copy-start.1
  209.1 7.4 copy-start
  239.6 2.8 copy-start.1
  257.5 7.4 copy-start
  288.1 2.8 copy-start.1
  306.0 7.4 copy-start
  336.5 2.8 copy-start.1
  354.4 7.4 copy-start
  385.0 2.8 copy-start.1
  402.9 7.4 copy-start
  433.5 2.8 copy-start.1
  451.4 7.4 copy-start
  481.9 2.8 copy-start.1
  505.3 1.6 copy-start.2
  505.3 390.0 %all-reduce.7.cloned.1.call-start = ((), (), s32[]{:S(2)}) async-start(), calls=%async_computation.3 | async-start | bytes 8192000
  510.5 0.7 copy-start.4
  510.5 1.3 copy-start.3
Sparse Core Ops, SparseCore 0:
  9.2 42.3 all-gather.4
  54.2 99.0 all-gather.6
  505.4 175.6 all-reduce.4
  683.6 211.6 all-reduce.6
where the time goes:
time: 910 us; the launch traced here: 906 us
  waiting for transfers between devices  526 us (58%)
  matrix products  160 us (18%)
  local copies, waits for them, and re-layouts  135 us (15%)
  other arithmetic  38.4 us (4%)
  loops' own time  33.8 us (4%)
  between operations  13.2 us (1%)
    unnamed x6, waiting for transfers between devices  384 us
    dot_general x140, matrix products, contract(): jnp.einsum(pattern, operator, values, precision=lax.Precision.HIGHEST, pr...  151 us
    all_gather x1, waiting for transfers between devices, shards(): column_block = lax.all_gather(orbitals, 'row', axis=0, tiled=True)  99.3 us
    dynamic_update_slice x14, local copies, waits for them, and re-layouts, set_row(): lax.dynamic_update_index_in_dim(terms_block, values[None, :], slot, 0)  83.5 us
    all_gather x1, waiting for transfers between devices, shards(): row_block = lax.all_gather(orbitals, 'col', axis=0, tiled=True)  41.9 us
    another operation x1, loops' own time, shards(): lax.fori_loop(0, pair_total, visit_pair, (empty_terms, empty_terms))  33.8 us
  transfers between devices with their start and end apart: 4, of which 4 were waited for; matrix products, arithmetic and copies ran while one was open for 1% of the time, Pallas kernels for 0%

commit v1 on v0

v1 whole, which is shorter than its diff:
```python
import functools

import jax
import jax.numpy as jnp
import ml_dtypes
import numpy as np
from jax import lax
from jax.experimental import pallas as pl
from jax.experimental.pallas import tpu as pltpu
from jax.sharding import PartitionSpec as P

GX = 40
PLANE = GX * GX
LANES = 1664
SLOTS = 8
ROWS = SLOTS * GX
NZ, NX = 8, 4
screen_width = 0.9
MESH = pl.DeviceIdType.MESH
F32, BF16 = jnp.float32, jnp.bfloat16


def split_np(a):
    high = a.astype(ml_dtypes.bfloat16)
    low = (a - high.astype(np.float64)).astype(ml_dtypes.bfloat16)
    return high, low


@functools.cache
def tables():
    n = np.arange(GX)
    phase = 2.0 * np.pi * ((n[:, None] * n[None, :]) % GX) / GX
    hartley = (np.cos(phase) + np.sin(phase)) / np.sqrt(GX)
    plane = np.zeros((LANES, LANES))
    plane[:PLANE, :PLANE] = np.kron(hartley, hartley)
    plane_high, plane_low = split_np(plane)
    high, low = split_np(np.kron(np.eye(2), hartley))
    along = np.concatenate([high, high, low], axis=1)
    signed = np.where(n < GX // 2, n, n - GX) * (2.0 * np.pi / GX)
    squared = signed**2
    total = squared[:, None, None] + squared[None, :, None] + squared[None, None, :]
    safe = np.where(total > 0, total, 1.0)
    screened = 4.0 * np.pi * (1.0 - np.exp(-safe / (4.0 * screen_width**2))) / safe
    kernel = np.where(total > 0, screened, np.pi / screen_width**2).reshape(GX, PLANE)
    padded = np.zeros((GX, LANES), np.float32)
    padded[:, :PLANE] = kernel
    return plane_high, plane_low, along, padded


def split(x):
    high = x.astype(BF16)
    return high, (x - high.astype(F32)).astype(BF16)


def places():
    r, c = lax.axis_index("row"), lax.axis_index("col")
    z, yh = r // 2, r % 2
    x, yl, core = c // 4, (c // 2) % 2, c % 2

    def row_of(dz, y):
        return ((z + dz + NZ) % NZ) * 2 + y

    def col_of(dx, y, k):
        return ((x + dx + NX) % NX) * 4 + y * 2 + k

    ids = {
        "z+": (row_of(1, yh), c),
        "z-": (row_of(-1, yh), c),
        "yh": (row_of(0, 1 - yh), c),
        "x+": (r, col_of(1, yl, core)),
        "x-": (r, col_of(-1, yl, core)),
        "yl": (r, col_of(0, 1 - yl, core)),
        "core": (r, col_of(0, yl, 1 - core)),
    }
    return r, c, yh, yl, core, row_of, col_of, ids


def greet(ids):
    barrier = pltpu.get_barrier_semaphore()
    for device in ids.values():
        pl.semaphore_signal(barrier, inc=1, device_id=device, device_id_type=MESH)
    pl.semaphore_wait(barrier, len(ids))


class Wires:
    def __init__(self, send_sem, recv_sem):
        self.send_sem, self.recv_sem, self.count = send_sem, recv_sem, 0

    def start(self, source, target, device):
        at = self.count
        self.count += 1
        copy = pltpu.make_async_remote_copy(
            src_ref=source,
            dst_ref=target,
            send_sem=self.send_sem.at[at],
            recv_sem=self.recv_sem.at[at],
            device_id=device,
            device_id_type=MESH,
        )
        copy.start()
        return copy


GATHER_COPIES = 30


def gather_kernel(own, col_block, row_block, send_sem, recv_sem, local_sem):
    r, c, yh, yl, core, row_of, col_of, ids = places()
    greet(ids)
    wires = Wires(send_sem, recv_sem)
    copies = []

    def send(block, index, source, where):
        copy = wires.start(source, block.at[index], ids[where])
        copies.append(copy)
        return copy

    local = [
        pltpu.make_async_copy(own, col_block.at[r], local_sem.at[0]),
        pltpu.make_async_copy(own, row_block.at[c], local_sem.at[1]),
    ]
    for copy in local:
        copy.start()
    col_b, row_b = col_block, row_block
    partner = send(col_b, r, own, "yh")
    plus_own = send(col_b, r, own, "z+")
    minus_own = send(col_b, r, own, "z-")
    mate = send(row_b, c, own, "yl")
    x_plus_own = send(row_b, c, own, "x+")
    x_minus_own = send(row_b, c, own, "x-")
    to_core = [send(row_b, c, own, "core")]

    partner.wait_recv()
    other = row_of(0, 1 - yh)
    plus_other = send(col_b, other, col_b.at[other], "z+")
    minus_other = send(col_b, other, col_b.at[other], "z-")
    mate.wait_recv()
    other_c = col_of(0, 1 - yl, core)
    x_plus_other = send(row_b, other_c, row_b.at[other_c], "x+")
    x_minus_other = send(row_b, other_c, row_b.at[other_c], "x-")
    to_core.append(send(row_b, other_c, row_b.at[other_c], "core"))

    def forward_x(first, second, sign, where):
        first.wait_recv()
        mine = col_of(-sign, yl, core)
        to_core.append(send(row_b, mine, row_b.at[mine], "core"))
        second.wait_recv()
        theirs = col_of(-sign, 1 - yl, core)
        to_core.append(send(row_b, theirs, row_b.at[theirs], "core"))
        lane = col_of(-sign, 0 if sign > 0 else 1, core)
        return send(row_b, lane, row_b.at[lane], where)

    def forward_z(first, second, step, sign, where):
        first.wait_recv()
        mine = row_of(-sign * step, yh)
        a = send(col_b, mine, col_b.at[mine], where)
        second.wait_recv()
        theirs = row_of(-sign * step, 1 - yh)
        b = send(col_b, theirs, col_b.at[theirs], where)
        return a, b

    plus = forward_z(plus_own, plus_other, 1, 1, "z+")
    minus = forward_z(minus_own, minus_other, 1, -1, "z-")
    x_far_plus = forward_x(x_plus_own, x_plus_other, 1, "x+")
    x_far_minus = forward_x(x_minus_own, x_minus_other, -1, "x-")
    plus = forward_z(*plus, 2, 1, "z+")
    minus = forward_z(*minus, 2, -1, "z-")
    x_far_plus.wait_recv()
    far = col_of(2, 0, core)
    to_core.append(send(row_b, far, row_b.at[far], "core"))
    x_far_minus.wait_recv()
    far = col_of(2, 1, core)
    to_core.append(send(row_b, far, row_b.at[far], "core"))
    for copy in plus + minus:
        copy.wait_recv()
    far = row_of(-3, 0)
    last_plus = send(col_b, far, col_b.at[far], "z+")
    far = row_of(3, 1)
    last_minus = send(col_b, far, col_b.at[far], "z-")
    for copy in to_core:
        copy.wait_recv()
    last_plus.wait_recv()
    last_minus.wait_recv()
    for copy in copies:
        copy.wait_send()
    for copy in local:
        copy.wait()


TILES = tuple((j * 256, 256) for j in range(6)) + ((1536, 128),)


def over_tiles(body):
    def step(j, carry):
        body(pl.multiple_of(j * 256, 256), 256)
        return carry

    lax.fori_loop(0, LANES // 256, step, 0)
    body(LANES - 128, 128)


def compute_kernel(
    pair_list, pair_count, global_places, col_block, row_block, plane_high, plane_low, along,
    kernel, first_fields, second_fields, density, spectrum, potential
):
    first_fields[...] = jnp.zeros_like(first_fields)
    second_fields[...] = jnp.zeros_like(second_fields)
    row_at, col_at = global_places[0], global_places[1]
    firsts = [pair_list[2 * p] for p in range(SLOTS)]
    seconds = [pair_list[2 * p + 1] for p in range(SLOTS)]
    count = pair_count[0]

    for q in range(SLOTS // 2):
        def wave(p):
            return row_block[firsts[p]].astype(F32) * col_block[seconds[p]].astype(F32)

        both = jnp.concatenate([wave(2 * q), wave(2 * q + 1)], axis=0)
        high, low = split(both)
        density[pl.ds(80 * q, 80), :] = high
        density[pl.ds(ROWS + 80 * q, 80), :] = low

    def plane_product(values, at, width):
        lanes = pl.ds(at, width)
        wide = jnp.dot(values[...], plane_high[:, lanes], preferred_element_type=F32)
        thin = jnp.dot(values[pl.ds(0, ROWS), :], plane_low[:, lanes], preferred_element_type=F32)
        return wide[:ROWS] + wide[ROWS:] + thin

    def along_x(part):
        high, low = split(part)
        stacked = jnp.concatenate([high, low, high], axis=0)
        return jnp.dot(along[...], stacked, preferred_element_type=F32)

    def forward(at, width):
        lanes = pl.ds(at, width)
        turned = plane_product(density, at, width)
        table = kernel[:, lanes]
        table = jnp.concatenate([table, table], axis=0)
        for q in range(SLOTS // 2):
            part = along_x(turned[80 * q : 80 * q + 80]) * table
            high, low = split(along_x(part))
            spectrum[pl.ds(80 * q, 80), lanes] = high
            spectrum[pl.ds(ROWS + 80 * q, 80), lanes] = low

    over_tiles(forward)

    def backward(at, width):
        lanes = pl.ds(at, width)
        potential[:, pl.ds(0, width)] = plane_product(spectrum, at, width)
        for p in range(SLOTS):
            f, s = firsts[p], seconds[p]
            live = jnp.where(p < count, 1.0, 0.0).astype(F32)
            same = (row_at * 16 + f) == (s * 16 + col_at)
            mirrored = jnp.where(same, 0.0, live).astype(F32)
            field = potential[pl.ds(GX * p, GX), pl.ds(0, width)]
            first_fields[f, :, lanes] += (live * field) * col_block[s, :, lanes].astype(F32)
            second_fields[s, :, lanes] += (mirrored * field) * row_block[f, :, lanes].astype(F32)

    over_tiles(backward)


SCATTER_COPIES = 30


def scatter_kernel(first_fields, second_fields, out, sent, received, send_sem, recv_sem):
    r, c, yh, yl, core, row_of, col_of, ids = places()
    greet(ids)
    wires = Wires(send_sem, recv_sem)
    copies = []
    terms = second_fields
    next_sent = [0]

    def send(source, where):
        at = wires.count
        copy = wires.start(source, received.at[at], ids[where])
        copies.append(copy)
        return copy, at

    def arrived(message):
        message[0].wait_recv()
        return received[message[1]]

    def send_value(value, where):
        slot = next_sent[0]
        next_sent[0] += 1
        sent[slot] = value
        return send(sent.at[slot], where)

    m0 = send(terms.at[row_of(4, 0)], "z+")
    n0 = send(terms.at[row_of(-4, 1)], "z-")
    m2 = send(terms.at[row_of(3, 1)], "z+")
    n2 = send(terms.at[row_of(-3, 0)], "z-")
    order = [(2, 0), (2, 1), (1, 0), (1, 1), (-1, 0), (-1, 1), (0, 0), (0, 1)]
    swaps = {
        key: send(first_fields.at[col_of(key[0], key[1], 1 - core)], "core") for key in order
    }

    def chip_sum(key):
        return first_fields[col_of(key[0], key[1], core)] + arrived(swaps[key])

    q0 = send_value(chip_sum((2, 0)), "x+")
    s0 = send_value(chip_sum((2, 1)), "x-")
    q2 = send_value(chip_sum((1, 1)), "x+")
    s2 = send_value(chip_sum((-1, 0)), "x-")
    m1 = send_value(terms[row_of(3, 0)] + arrived(m0), "z+")
    n1 = send_value(terms[row_of(-3, 1)] + arrived(n0), "z-")
    m4 = send_value(terms[row_of(2, 1)] + arrived(m2), "z+")
    n4 = send_value(terms[row_of(-2, 0)] + arrived(n2), "z-")
    q1 = send_value(chip_sum((1, 0)) + arrived(q0), "x+")
    s1 = send_value(chip_sum((-1, 1)) + arrived(s0), "x-")
    m3 = send_value(terms[row_of(2, 0)] + arrived(m1), "z+")
    n3 = send_value(terms[row_of(-2, 1)] + arrived(n1), "z-")
    m6 = send_value(terms[row_of(1, 1)] + arrived(m4), "z+")
    n6 = send_value(terms[row_of(-1, 0)] + arrived(n4), "z-")
    low = sent.shape[0] - 2
    high = sent.shape[0] - 1
    sent[low] = chip_sum((0, 0)) + arrived(q1) + arrived(s2)
    sent[high] = chip_sum((0, 1)) + arrived(q2) + arrived(s1)
    last_x = send(sent.at[low + 1 - yl], "yl")
    m5 = send_value(terms[row_of(1, 0)] + arrived(m3), "z+")
    n5 = send_value(terms[row_of(-1, 1)] + arrived(n3), "z-")
    out[...] = sent[low + yl] + arrived(last_x)
    last_x[0].wait_send()
    sent[low] = terms[row_of(0, 0)] + arrived(m5) + arrived(n6)
    sent[high] = terms[row_of(0, 1)] + arrived(m6) + arrived(n5)
    last_z = send(sent.at[low + 1 - yh], "yh")
    out[...] += sent[low + yh]
    out[...] += arrived(last_z)
    for copy in copies:
        if copy is not last_x[0]:
            copy.wait_send()


def shards(orbitals, pair_list, pair_count):
    vmem = pl.BlockSpec(memory_space=pltpu.VMEM)
    smem = pl.BlockSpec(memory_space=pltpu.SMEM)
    anywhere = pl.BlockSpec(memory_space=pl.ANY)
    plane_high, plane_low, along, kernel = (jnp.asarray(t) for t in tables())
    own = jnp.pad(orbitals.reshape(GX, PLANE), ((0, 0), (0, LANES - PLANE)))
    block = jax.ShapeDtypeStruct((16, GX, LANES), BF16)
    col_block, row_block = pl.pallas_call(
        gather_kernel,
        out_shape=(block, block),
        in_specs=[anywhere],
        out_specs=(anywhere, anywhere),
        scratch_shapes=[
            pltpu.SemaphoreType.DMA((GATHER_COPIES,)),
            pltpu.SemaphoreType.DMA((GATHER_COPIES,)),
            pltpu.SemaphoreType.DMA((2,)),
        ],
        compiler_params=pltpu.CompilerParams(collective_id=0, has_side_effects=True),
        name="gather",
    )(own)
    at = jnp.stack([lax.axis_index("row"), lax.axis_index("col")]).astype(jnp.int32)
    fields = jax.ShapeDtypeStruct((16, GX, LANES), F32)
    first_fields, second_fields = pl.pallas_call(
        compute_kernel,
        out_shape=(fields, fields),
        in_specs=[smem] * 3 + [vmem] * 6,
        out_specs=(vmem, vmem),
        scratch_shapes=[
            pltpu.VMEM((2 * ROWS, LANES), BF16),
            pltpu.VMEM((2 * ROWS, LANES), BF16),
            pltpu.VMEM((ROWS, 256), F32),
        ],
        compiler_params=pltpu.CompilerParams(vmem_limit_bytes=56 * 1024 * 1024),
        name="pairs",
    )(pair_list.reshape(-1), pair_count, at, col_block, row_block, plane_high, plane_low, along, kernel)
    total = pl.pallas_call(
        scatter_kernel,
        out_shape=jax.ShapeDtypeStruct((GX, LANES), F32),
        in_specs=[vmem, vmem],
        out_specs=vmem,
        scratch_shapes=[
            pltpu.VMEM((18, GX, LANES), F32),
            pltpu.VMEM((SCATTER_COPIES, GX, LANES), F32),
            pltpu.SemaphoreType.DMA((SCATTER_COPIES,)),
            pltpu.SemaphoreType.DMA((SCATTER_COPIES,)),
        ],
        compiler_params=pltpu.CompilerParams(
            collective_id=1, has_side_effects=True, vmem_limit_bytes=56 * 1024 * 1024
        ),
        name="scatter",
    )(first_fields, second_fields)
    return total[:, :PLANE].reshape(1, GX * PLANE)


def solution(mesh):
    return jax.shard_map(
        shards,
        mesh=mesh,
        in_specs=(P(("row", "col"), None), P(("row", "col"), None, None), P(("row", "col"))),
        out_specs=P(("row", "col"), None),
        check_vma=False,
    )
```

time: 910 us -> 132 us (0.15)
  waiting for transfers between devices: 526 us -> 0 us
  matrix products: 160 us -> 0 us
  local copies, waits for them, and re-layouts: 135 us -> 4.14 us
  Pallas kernels: 0 us -> 123 us
  other arithmetic: 38.4 us -> 2.25 us
  loops' own time: 33.8 us -> 0 us
  between operations: 13.2 us -> 0.68 us
    unnamed x6 -> x0, waiting for transfers between devices: 384 us -> none
    dot_general x142 -> x0, matrix products: 160 us -> none  [the longest x140 151 us: contract(): jnp.einsum(pattern, operator, values, precision=lax.Precision.HIGHEST, pr...]
    all_gather x2 -> x0, waiting for transfers between devices: 141 us -> none  [the longest x1 99.3 us: shards(): column_block = lax.all_gather(orbitals, 'row', axis=0, tiled=True)]
    pallas_call x0 -> x3, Pallas kernels: none -> 123 us  [the longest x1 52.7 us: shards(): pl.pallas_call(scatter_kernel, out_shape=jax.ShapeDtypeStruct((GX, LANES)...]
    dynamic_update_slice x14 -> x0, local copies, waits for them, and re-layouts: 83.5 us -> none  [set_row(): lax.dynamic_update_index_in_dim(terms_block, values[None, :], slot, 0)]
    another operation x1 -> x0, loops' own time: 33.8 us -> none  [shards(): lax.fori_loop(0, pair_total, visit_pair, (empty_terms, empty_terms))]
    mul x15 -> x0, other arithmetic: 33 us -> none  [the longest x7 17.4 us: pair_terms(): distinct[pair_slot] * potential * first_wave]
    dynamic_slice x21 -> x0, local copies, waits for them, and re-layouts: 13.5 us -> none  [the longest x7 4.85 us: visit_pair(): first_row = first_local[pair_slot]]
  transfers between devices with their start and end apart: 4 -> 0, of which waited for: 4 -> 0; matrix products, arithmetic and copies ran while one was open for 1% -> 0% of each run, Pallas kernels for 0% -> 0%
where the time goes in v1:
time: 132 us; the launch traced here: 130 us
  Pallas kernels  123 us (93%)
  local copies, waits for them, and re-layouts  4.14 us (3%)
  other arithmetic  2.25 us (2%)
    pallas_call x1, Pallas kernels, shards(): pl.pallas_call(scatter_kernel, out_shape=jax.ShapeDtypeStruct((GX, LANES)...  52.7 us
    pallas_call x1, Pallas kernels, shards(): pl.pallas_call(gather_kernel, out_shape=(block, block), in_specs=[anywher...  38.9 us
    pallas_call x1, Pallas kernels, shards(): pl.pallas_call(compute_kernel, out_shape=(fields, fields), in_specs=[smem...  31.4 us

profile of v1, /device:TPU:8, one launch (start us, length us, event | category | flops | bytes accessed | tf_op | source)
XLA Modules:
  0.0 130.0 jit_solution(2231484206543557846)
XLA Ops:
  0.7 0.6 pad_add_fusion.global_places
  1.2 0.8 copy.9
  2.0 0.6 reshape.9.pair_list
  2.6 1.7 %reduce = bf16[64000]{0:T(1024)(128)(2,1)S(1)} reduce(bf16[1,64000]{1,0:T(2,128)(2,1)} %param.7, bf16[]{:T(256)} %constant.27), dimensions={0}, to_apply=%param.7.reduce_sub_computation | reduce | bytes 256002 | tf_op args[0]
  4.3 0.2 reshape.10
  4.4 0.7 pad.4.own
  5.1 38.9 %gather.1 = (bf16[16,40,1664]{2,1,0:T(8,128)(2,1)}, bf16[16,40,1664]{2,1,0:T(8,128)(2,1)}) custom-call(bf16[40,1664]{1,0:T(8,128)(2,1)} %pad.4.own), custom_call_target="tpu_custom_call" | custom-call | tf_op jit(solution)/shard_map/gather/pallas_call | solution.py:340
  44.0 31.4 %pairs.1 = (f32[16,40,1664]{2,1,0:T(8,128)}, f32[16,40,1664]{2,1,0:T(8,128)}) custom-call(s32[16]{0:T(128)} %reshape.9.pair_list, s32[1]{0:T(128)S(6)} %copy.10.pair_count, s32[2]{0:T(128)} %pad_add_fusion.global_places, bf16[16,40,1664]{2,1,0:T(8,128)(2,1)} %get-tuple-element.9.col_block, bf16[16,40,1664]{2,1,0:T(8,128)(2,1)} %get-tuple-element.10.row_block, ...), custom_call_target="tpu_custom_call" | custom-call | tf_op jit(solution)/shard_map/pairs/pallas_call | solution.py:355
  75.4 52.7 %scatter.1 = f32[40,1664]{1,0:T(8,128)} custom-call(f32[16,40,1664]{2,1,0:T(8,128)} %get-tuple-element.11.first_fields, f32[16,40,1664]{2,1,0:T(8,128)} %get-tuple-element.12.second_fields), custom_call_target="tpu_custom_call" | custom-call | tf_op jit(solution)/shard_map/scatter/pallas_call | solution.py:368
  128.1 1.9 %reshape.11 = f32[1,64000]{1,0:T(1,128)} reshape(f32[40,1600]{1,0:T(8,128)} %bitcast.3) | data formatting | bytes 512000 | tf_op jit(solution)/shard_map/reshape | solution.py:384

commit v2 on v0

v2 whole, which is shorter than its diff:
```python
import functools

import jax
import jax.numpy as jnp
import ml_dtypes
import numpy as np
from jax import lax
from jax.experimental import pallas as pl
from jax.experimental.pallas import tpu as pltpu
from jax.sharding import PartitionSpec as P

GX = 40
HALF = GX // 2
PART = HALF * GX
MAIN = 768
TAIL = PART - MAIN
WIDE = 2 * MAIN + 128
FOLD = MAIN + 128
SLOTS = 8
BANDS = 16
NZ, NX = 8, 4
SLAB_ROWS = (16, 16, 8)
SLAB_LANES = (WIDE, WIDE, FOLD)
SLABS = range(3)
screen_width = 0.9
MESH = pl.DeviceIdType.MESH
F32, BF16, I16 = jnp.float32, jnp.bfloat16, jnp.int16
TOP = 32767.0
GATHER_COPIES = 30
SCATTER_COPIES = 30
CODED = 22


def split_np(a):
    high = a.astype(ml_dtypes.bfloat16)
    low = (a - high.astype(np.float64)).astype(ml_dtypes.bfloat16)
    return high, low


@functools.cache
def tables():
    def cas(phase):
        return np.cos(phase) + np.sin(phase)

    n, h = np.arange(GX), np.arange(HALF)
    root = 1.0 / np.sqrt(GX)
    full = cas(2.0 * np.pi * np.outer(n, n) / GX) * root
    even = cas(2.0 * np.pi * np.outer(h, h) / HALF) * root
    odd = cas(2.0 * np.pi * np.outer(2 * h + 1, 2 * h + 1) / (4 * HALF)) * root
    plane = np.zeros((2, FOLD, FOLD))
    plane[0, :PART, :PART] = np.kron(even, full)
    plane[1, :PART, :PART] = np.kron(odd, full)
    plane_high, plane_low = split_np(plane)
    xs = np.concatenate([np.r_[a:b, a:b] for a, b in ((0, 16), (16, 32), (32, 40))])
    pair = np.concatenate([np.r_[[0] * k, [1] * k] for k in (16, 16, 8)])
    both = np.where(pair[:, None] == pair[None, :], full[xs][:, xs], 0.0)
    high, low = split_np(both)
    along = np.concatenate([high, high, low], axis=1)
    signed = np.where(n < GX // 2, n, n - GX) * (2.0 * np.pi / GX)
    squared = signed**2
    total = squared[:, None, None] + squared[None, :, None] + squared[None, None, :]
    safe = np.where(total > 0, total, 1.0)
    screened = 4.0 * np.pi * (1.0 - np.exp(-safe / (4.0 * screen_width**2))) / safe
    kernel = np.where(total > 0, screened, np.pi / screen_width**2)
    padded = np.zeros((GX, 2, FOLD), np.float32)
    padded[:, 0, :PART] = kernel[:, 0::2].reshape(GX, PART)
    padded[:, 1, :PART] = kernel[:, 1::2].reshape(GX, PART)
    return plane_high, plane_low, along, padded.reshape(GX, 2 * FOLD)[xs]


def split(x):
    high = x.astype(BF16)
    return high, (x - high.astype(F32)).astype(BF16)


def encode(value):
    most = jnp.max(jnp.abs(value), axis=1, keepdims=True)
    power = jnp.floor(jnp.log(jnp.maximum(most, 1e-30)) * 1.4426950408889634)
    share = value * (0.5 * jnp.exp2(-power))
    root = share * lax.rsqrt(jnp.maximum(jnp.abs(share), 1e-20))
    code = jnp.clip(jnp.round(root * TOP), -TOP, TOP)
    lanes = lax.broadcasted_iota(jnp.int32, (value.shape[0], 128), 1)
    last = jnp.where(lanes >= 64, power, code[:, -128:])
    return jnp.concatenate([code[:, :-128], last], axis=1).astype(jnp.int32).astype(I16)


def decode(code):
    wide = code.astype(jnp.int32).astype(F32)
    scale = jnp.exp2(wide[:, -64:-63]) * (2.0 / (TOP * TOP))
    return wide * jnp.abs(wide) * scale


def places():
    r, c = lax.axis_index("row"), lax.axis_index("col")
    z, yh = r // 2, r % 2
    x, yl, core = c // 4, (c // 2) % 2, c % 2

    def row_of(dz, y):
        return ((z + dz + NZ) % NZ) * 2 + y

    def col_of(dx, y, k):
        return ((x + dx + NX) % NX) * 4 + y * 2 + k

    ids = {
        "z+": (row_of(1, yh), c),
        "z-": (row_of(-1, yh), c),
        "yh": (row_of(0, 1 - yh), c),
        "x+": (r, col_of(1, yl, core)),
        "x-": (r, col_of(-1, yl, core)),
        "yl": (r, col_of(0, 1 - yl, core)),
        "core": (r, col_of(0, yl, 1 - core)),
    }
    return r, c, yh, yl, core, row_of, col_of, ids


def greet(ids):
    barrier = pltpu.get_barrier_semaphore()
    for device in ids.values():
        pl.semaphore_signal(barrier, inc=1, device_id=device, device_id_type=MESH)
    pl.semaphore_wait(barrier, len(ids))


class Wires:
    def __init__(self, send_sem, recv_sem, ids):
        self.send_sem, self.recv_sem, self.ids = send_sem, recv_sem, ids
        self.copies = []

    def start(self, source, target, where):
        at = len(self.copies)
        copy = pltpu.make_async_remote_copy(
            src_ref=source,
            dst_ref=target,
            send_sem=self.send_sem.at[at],
            recv_sem=self.recv_sem.at[at],
            device_id=self.ids[where],
            device_id_type=MESH,
        )
        copy.start()
        self.copies.append(copy)
        return copy


def gather_stages(wires, place, own, cols, rows):
    r, c, yh, yl, core, row_of, col_of, _ = place
    got = {}

    def send_col(name, index, where, source=None):
        got[name] = wires.start(cols.at[index] if source is None else source, cols.at[index], where)

    def send_row(name, index, where, source=None):
        got[name] = wires.start(rows.at[index] if source is None else source, rows.at[index], where)

    def stage0():
        send_col("yh", r, "yh", own)
        send_col("z+a", r, "z+", own)
        send_col("z-a", r, "z-", own)
        send_row("yl", c, "yl", own)
        send_row("x+a", c, "x+", own)
        send_row("x-a", c, "x-", own)
        send_row("k0", c, "core", own)

    def stage1():
        got["yh"].wait_recv()
        other = row_of(0, 1 - yh)
        send_col("z+b", other, "z+")
        send_col("z-b", other, "z-")
        got["yl"].wait_recv()
        other = col_of(0, 1 - yl, core)
        send_row("x+b", other, "x+")
        send_row("x-b", other, "x-")
        send_row("k1", other, "core")

    def forward_z(step):
        for sign, where in ((1, "z+"), (-1, "z-")):
            got[where + "a"].wait_recv()
            send_col(where + "a", row_of(-sign * step, yh), where)
        for sign, where in ((1, "z+"), (-1, "z-")):
            got[where + "b"].wait_recv()
            send_col(where + "b", row_of(-sign * step, 1 - yh), where)

    def stage2():
        forward_z(1)
        for sign, where, lane in ((1, "x+", 0), (-1, "x-", 1)):
            got[where + "a"].wait_recv()
            send_row("k2" + where, col_of(-sign, yl, core), "core")
            got[where + "b"].wait_recv()
            send_row("k3" + where, col_of(-sign, 1 - yl, core), "core")
            send_row(where + "c", col_of(-sign, lane, core), where)

    def stage3():
        forward_z(2)
        for where, lane in (("x+", 0), ("x-", 1)):
            got[where + "c"].wait_recv()
            send_row("k4" + where, col_of(2, lane, core), "core")

    def stage4():
        for name in ("z+a", "z-a", "z+b", "z-b"):
            got[name].wait_recv()
        send_col("z+c", row_of(-3, 0), "z+")
        send_col("z-c", row_of(3, 1), "z-")

    def stage5():
        for name in ("z+c", "z-c", "k0", "k1", "k2x+", "k3x+", "k2x-", "k3x-", "k4x+", "k4x-"):
            got[name].wait_recv()

    return [stage0, stage1, stage2, stage3, stage4, stage5]


def scatter_stages(wires, place, first_at, second_at, firsts, seconds, coded, codes_in, swapped, swaps_in, store):
    r, c, yh, yl, core, row_of, col_of, _ = place
    got, used = {}, [0]

    def term(index):
        return seconds[second_at(index)]

    def send(name, value, where):
        slot = used[0]
        used[0] += 1
        coded[slot] = encode(value)
        got[name] = (wires.start(coded.at[slot], codes_in.at[slot], where), slot)

    def arrived(name):
        copy, slot = got[name]
        copy.wait_recv()
        return decode(codes_in[slot])

    order = [(2, 0), (2, 1), (1, 1), (-1, 0), (1, 0), (-1, 1), (0, 0), (0, 1)]

    def stage0():
        send("m0", term(row_of(4, 0)), "z+")
        send("n0", term(row_of(-4, 1)), "z-")
        for slot, (dx, y) in enumerate(order):
            swapped[slot] = firsts[first_at(col_of(dx, y, 1 - core))]
            got[dx, y] = (wires.start(swapped.at[slot], swaps_in.at[slot], "core"), slot)
        send("m2", term(row_of(3, 1)), "z+")
        send("n2", term(row_of(-3, 0)), "z-")

    def chip_sum(key):
        copy, slot = got[key]
        copy.wait_recv()
        return firsts[first_at(col_of(key[0], key[1], core))] + swaps_in[slot]

    def stage1():
        send("q0", chip_sum((2, 0)), "x+")
        send("s0", chip_sum((2, 1)), "x-")
        send("m1", term(row_of(3, 0)) + arrived("m0"), "z+")
        send("n1", term(row_of(-3, 1)) + arrived("n0"), "z-")
        send("q2", chip_sum((1, 1)), "x+")
        send("s2", chip_sum((-1, 0)), "x-")
        send("m4", term(row_of(2, 1)) + arrived("m2"), "z+")
        send("n4", term(row_of(-2, 0)) + arrived("n2"), "z-")

    def stage2():
        send("q1", chip_sum((1, 0)) + arrived("q0"), "x+")
        send("s1", chip_sum((-1, 1)) + arrived("s0"), "x-")
        send("m3", term(row_of(2, 0)) + arrived("m1"), "z+")
        send("n3", term(row_of(-2, 1)) + arrived("n1"), "z-")
        send("m6", term(row_of(1, 1)) + arrived("m4"), "z+")
        send("n6", term(row_of(-1, 0)) + arrived("n4"), "z-")

    def halves(pair, mine):
        swap = jnp.where(mine == 0, 1.0, 0.0).astype(F32)
        keep = 1.0 - swap
        return swap * pair[0] + keep * pair[1], keep * pair[0] + swap * pair[1]

    kept = {}

    def stage3():
        send("m5", term(row_of(1, 0)) + arrived("m3"), "z+")
        send("n5", term(row_of(-1, 1)) + arrived("n3"), "z-")
        pair = [
            chip_sum((0, 0)) + arrived("q1") + arrived("s2"),
            chip_sum((0, 1)) + arrived("q2") + arrived("s1"),
        ]
        mine, other = halves(pair, yl)
        store(mine, False)
        send("x", other, "yl")

    def stage4():
        pair = [
            term(row_of(0, 0)) + arrived("m5") + arrived("n6"),
            term(row_of(0, 1)) + arrived("m6") + arrived("n5"),
        ]
        mine, other = halves(pair, yh)
        store(mine, True)
        send("z", other, "yh")
        store(arrived("x"), True)

    def stage5():
        store(arrived("z"), True)

    return [stage0, stage1, stage2, stage3, stage4, stage5]


def fold(rho, slab):
    rows = SLAB_ROWS[slab]
    if rows == 16:
        near, far, tail = rho[:, :MAIN], rho[:, MAIN : 2 * MAIN], rho[:, 2 * MAIN :]
    else:
        near, far, tail = rho[:rows, :MAIN], rho[rows:, :MAIN], rho[:rows, MAIN:]
    moved = pltpu.roll(tail, 128 - TAIL, 1)
    even = jnp.concatenate([near + far, tail + moved], axis=1)
    return even, jnp.concatenate([near - far, tail - moved], axis=1)


def exchange_kernel(
    own, pair_list, pair_count, plane_high_in, plane_low_in, along, kernel, out,
    own_0, own_1, own_2, cols_0, cols_1, cols_2, rows_0, rows_1, rows_2,
    dens_0, dens_1, dens_2, spec_0, spec_1, spec_2, first_0, first_1, first_2,
    second_0, second_1, second_2, coded_0, coded_1, coded_2, codes_in_0, codes_in_1, codes_in_2,
    swapped_0, swapped_1, swapped_2, swaps_in_0, swaps_in_1, swaps_in_2,
    plane_high, plane_low, send_sem, recv_sem, local_sem,
):
    owns, cols, rows = (own_0, own_1, own_2), (cols_0, cols_1, cols_2), (rows_0, rows_1, rows_2)
    dens, spec = (dens_0, dens_1, dens_2), (spec_0, spec_1, spec_2)
    first_sums, second_sums = (first_0, first_1, first_2), (second_0, second_1, second_2)
    coded, codes_in = (coded_0, coded_1, coded_2), (codes_in_0, codes_in_1, codes_in_2)
    swapped, swaps_in = (swapped_0, swapped_1, swapped_2), (swaps_in_0, swaps_in_1, swaps_in_2)
    place = places()
    r, c, ids = place[0], place[1], place[-1]

    local = [
        pltpu.make_async_copy(plane_high_in, plane_high, local_sem.at[0]),
        pltpu.make_async_copy(plane_low_in, plane_low, local_sem.at[1]),
    ]
    own_0[...] = own[pl.ds(0, 16), :]
    own_1[...] = own[pl.ds(16, 16), :]
    rest = own[pl.ds(32, 8), :].astype(F32)
    low_rows = jnp.concatenate([rest[:, MAIN : 2 * MAIN], jnp.zeros((8, 128), F32)], axis=1)
    high_rows = jnp.concatenate([rest[:, :MAIN], rest[:, 2 * MAIN :]], axis=1)
    own_2[...] = jnp.concatenate([high_rows, low_rows], axis=0).astype(BF16)
    greet(ids)
    wires = Wires(send_sem, recv_sem, ids)
    keeps = []
    for k in SLABS:
        keeps.append(pltpu.make_async_copy(owns[k], cols[k].at[r], local_sem.at[2 + 2 * k]))
        keeps.append(pltpu.make_async_copy(owns[k], rows[k].at[c], local_sem.at[3 + 2 * k]))
    gather = [gather_stages(wires, place, owns[k], cols[k], rows[k]) for k in SLABS]

    firsts = [pair_list[0, p, 0] for p in range(SLOTS)]
    seconds = [pair_list[0, p, 1] for p in range(SLOTS)]
    count = pair_count[0]
    first_band = [jnp.where(p < count, firsts[p], -1) for p in range(SLOTS)]
    second_band = [
        jnp.where((p < count) & (r * BANDS + firsts[p] != seconds[p] * BANDS + c), seconds[p], -1)
        for p in range(SLOTS)
    ]

    def last_slot(bands, wanted):
        at = SLOTS
        for p, band in enumerate(bands):
            at = jnp.where(band == wanted, p, at)
        return at

    before_first = [last_slot(first_band[:p], first_band[p]) for p in range(SLOTS)]
    before_second = [last_slot(second_band[:p], second_band[p]) for p in range(SLOTS)]

    def density(k, p):
        return rows[k][firsts[p]].astype(F32) * cols[k][seconds[p]].astype(F32)

    def fill(k, slots):
        size = SLAB_ROWS[k]
        group = 16 // size
        for p in range(slots[0], slots[1], group):
            parts = [fold(density(k, p + i), k) for i in range(group)]
            for parity in range(2):
                value = jnp.concatenate([part[parity] for part in parts], axis=0)
                high, low = split(value)
                dens[k][parity, pl.ds(p * size, 16), :] = high
                dens[k][parity, pl.ds((SLOTS + p) * size, 16), :] = low

    def product(values, parity, at, width):
        lanes = pl.ds(at, width)
        half = values.shape[0] // 2
        wide = jnp.dot(values, plane_high[parity, :, lanes], preferred_element_type=F32)
        thin = jnp.dot(values[:half], plane_low[parity, :, lanes], preferred_element_type=F32)
        return wide[:half] + wide[half:] + thin

    def forward(k, parity, at, width):
        size = SLOTS * SLAB_ROWS[k]
        high, low = split(product(dens[k][parity], parity, at, width))
        lanes = pl.ds(parity * FOLD + at, width)
        spec[k][pl.ds(0, size), lanes] = high
        spec[k][pl.ds(size, size), lanes] = low

    def forward_pieces(k):
        pieces = [functools.partial(fill, k, (0, 4)), functools.partial(fill, k, (4, 8))]
        for parity in range(2):
            for at, width in ((0, 512), (512, 384)):
                pieces.append(functools.partial(forward, k, parity, at, width))
        return pieces

    def along_x(part):
        high, low = split(part)
        return jnp.dot(along[...], jnp.concatenate([high, low, high], axis=0), preferred_element_type=F32)

    def middle(j, carry):
        lanes = pl.ds(pl.multiple_of(j * 256, 256), 256)
        table = kernel[:, lanes]
        for q in range(SLOTS // 2):
            def rows_of(shift):
                return [spec[k][pl.ds((shift * SLOTS + 2 * q) * SLAB_ROWS[k], 2 * SLAB_ROWS[k]), lanes] for k in SLABS]

            high, low = rows_of(0), rows_of(1)
            turned = jnp.dot(along[...], jnp.concatenate(high + low + high, axis=0), preferred_element_type=F32)
            high, low = split(along_x(turned * table))
            at = 0
            for k in SLABS:
                size = 2 * SLAB_ROWS[k]
                spec[k][pl.ds(q * size, size), lanes] = high[at : at + size]
                spec[k][pl.ds(SLOTS * SLAB_ROWS[k] + q * size, size), lanes] = low[at : at + size]
                at += size
        return carry

    def backward(k, at, width):
        size = SLAB_ROWS[k]
        even = product(spec[k][:, pl.ds(0, FOLD)], 0, at, width)
        odd = product(spec[k][:, pl.ds(FOLD, FOLD)], 1, at, width)
        near, far = even + odd, even - odd
        if at == MAIN:
            lane = lax.broadcasted_iota(jnp.int32, near.shape, 1)
            near = jnp.where(lane < TAIL, near, pltpu.roll(far, TAIL, 1))
        for p in range(SLOTS):
            mine = slice(p * size, (p + 1) * size)
            if at == MAIN:
                spans = [(WIDE - 128 if size == 16 else MAIN, near[mine])]
                if size < 16:
                    spans = [(MAIN, jnp.concatenate([near[mine], jnp.zeros_like(near[mine])], axis=0))]
            elif size == 16:
                spans = [(at, near[mine]), (MAIN + at, far[mine])]
            else:
                spans = [(at, jnp.concatenate([near[mine], far[mine]], axis=0))]
            for start, value in spans:
                lanes = pl.ds(start, width)
                to_first = value * cols[k][seconds[p], :, lanes].astype(F32)
                to_second = value * rows[k][firsts[p], :, lanes].astype(F32)
                first_sums[k][p, :, lanes] = to_first + first_sums[k][before_first[p], :, lanes]
                second_sums[k][p, :, lanes] = to_second + second_sums[k][before_second[p], :, lanes]

    def backward_pieces(k):
        return [functools.partial(backward, k, at, width) for at, width in ((0, 256), (256, 256), (512, 256), (768, 128))]

    def store(k, value, more):
        if SLAB_ROWS[k] == 16:
            spans = [(slice(16 * k, 16 * k + 16), slice(0, WIDE), value)]
        else:
            spans = [
                (slice(32, 40), slice(0, MAIN), value[:8, :MAIN]),
                (slice(32, 40), slice(MAIN, 2 * MAIN), value[8:, :MAIN]),
                (slice(32, 40), slice(2 * MAIN, WIDE), value[:8, MAIN:]),
            ]
        for some_rows, lanes, part in spans:
            out[some_rows, lanes] = out[some_rows, lanes] + part if more else part

    scatter = [
        scatter_stages(
            wires, place, functools.partial(last_slot, first_band), functools.partial(last_slot, second_band),
            first_sums[k], second_sums[k], coded[k], codes_in[k], swapped[k], swaps_in[k],
            functools.partial(store, k),
        )
        for k in SLABS
    ]

    def run(steps):
        for step in steps:
            step()

    def mixed(pieces, stages):
        done = 0
        for i, piece in enumerate(pieces):
            piece()
            while done * len(pieces) < (i + 1) * len(stages) and done < len(stages):
                stages[done]()
                done += 1

    a, b, d = gather
    a[0]()
    for copy in keeps:
        copy.start()
    b[0]()
    for copy in local:
        copy.start()
    run([a[1], d[0], a[2], b[1], a[3], b[2], a[4], d[1], b[3]])
    for k in SLABS:
        first_sums[k][SLOTS] = jnp.zeros(first_sums[k].shape[1:], F32)
        second_sums[k][SLOTS] = jnp.zeros(second_sums[k].shape[1:], F32)
    run([d[2], a[5]])
    for copy in local:
        copy.wait()
    for copy in keeps:
        copy.wait()
    mixed(forward_pieces(0), [b[4], d[3], d[4]])
    b[5]()
    mixed(forward_pieces(1), [])
    d[5]()
    mixed(forward_pieces(2), [])
    lax.fori_loop(0, 2 * FOLD // 256, middle, 0)
    a, b, d = scatter
    run(backward_pieces(0))
    a[0]()
    mixed(backward_pieces(1), [a[1]])
    b[0]()
    mixed(backward_pieces(2), [a[2], b[1]])
    run([d[0], a[3], b[2], d[1], a[4], b[3], d[2], a[5], b[4], d[3], b[5], d[4], d[5]])
    for copy in wires.copies:
        copy.wait_send()


def exchange(own, pair_list, pair_count):
    vmem = pl.BlockSpec(memory_space=pltpu.VMEM)
    smem = pl.BlockSpec(memory_space=pltpu.SMEM)
    anywhere = pl.BlockSpec(memory_space=pl.ANY)
    plane_high, plane_low, along, kernel = (jnp.asarray(t) for t in tables())

    def each(shape, kind):
        return [pltpu.VMEM(shape(k), kind) for k in SLABS]

    def stack(count):
        return lambda k: (count, 16, SLAB_LANES[k])

    copies = len(SLAB_ROWS) * (GATHER_COPIES + SCATTER_COPIES)
    return pl.pallas_call(
        exchange_kernel,
        out_shape=jax.ShapeDtypeStruct((GX, WIDE), F32),
        in_specs=[vmem, smem, smem, anywhere, anywhere, vmem, vmem],
        out_specs=vmem,
        scratch_shapes=[
            *each(lambda k: (16, SLAB_LANES[k]), BF16),
            *each(stack(BANDS), BF16),
            *each(stack(BANDS), BF16),
            *each(lambda k: (2, 2 * SLOTS * SLAB_ROWS[k], FOLD), BF16),
            *each(lambda k: (2 * SLOTS * SLAB_ROWS[k], 2 * FOLD), BF16),
            *each(stack(SLOTS + 1), F32),
            *each(stack(SLOTS + 1), F32),
            *each(stack(CODED), I16),
            *each(stack(CODED), I16),
            *each(stack(SLOTS), F32),
            *each(stack(SLOTS), F32),
            pltpu.VMEM(plane_high.shape, BF16),
            pltpu.VMEM(plane_low.shape, BF16),
            pltpu.SemaphoreType.DMA((copies,)),
            pltpu.SemaphoreType.DMA((copies,)),
            pltpu.SemaphoreType.DMA((8,)),
        ],
        compiler_params=pltpu.CompilerParams(
            collective_id=0, has_side_effects=True, vmem_limit_bytes=52 * 1024 * 1024
        ),
        name="exchange",
    )(own, pair_list, pair_count, plane_high, plane_low, along, kernel)


def shards(orbitals, pair_list, pair_count):
    halves = orbitals.reshape(GX, 2, PART)
    own = jnp.concatenate(
        [halves[:, 0, :MAIN], halves[:, 1, :MAIN], halves[:, 0, MAIN:], halves[:, 1, MAIN:], jnp.zeros((GX, 64), BF16)],
        axis=1,
    )
    fields = exchange(own, pair_list, pair_count)
    near = [fields[:, :MAIN], fields[:, 2 * MAIN : 2 * MAIN + TAIL]]
    far = [fields[:, MAIN : 2 * MAIN], fields[:, 2 * MAIN + TAIL : 2 * MAIN + 2 * TAIL]]
    return jnp.concatenate(near + far, axis=1).reshape(1, GX * GX * GX)


def solution(mesh):
    return jax.shard_map(
        shards,
        mesh=mesh,
        in_specs=(P(("row", "col"), None), P(("row", "col"), None, None), P(("row", "col"))),
        out_specs=P(("row", "col"), None),
        check_vma=False,
    )
```

time: 910 us -> 88.3 us (0.10)
  waiting for transfers between devices: 526 us -> 0 us
  matrix products: 160 us -> 0 us
  local copies, waits for them, and re-layouts: 135 us -> 4.36 us
  Pallas kernels: 0 us -> 80.8 us
  other arithmetic: 38.4 us -> 1.66 us
  loops' own time: 33.8 us -> 0 us
  between operations: 13.2 us -> 0.72 us
    unnamed x6 -> x0, waiting for transfers between devices: 384 us -> none
    dot_general x142 -> x0, matrix products: 160 us -> none  [the longest x140 151 us: contract(): jnp.einsum(pattern, operator, values, precision=lax.Precision.HIGHEST, pr...]
    all_gather x2 -> x0, waiting for transfers between devices: 141 us -> none  [the longest x1 99.3 us: shards(): column_block = lax.all_gather(orbitals, 'row', axis=0, tiled=True)]
    dynamic_update_slice x14 -> x0, local copies, waits for them, and re-layouts: 83.5 us -> none  [set_row(): lax.dynamic_update_index_in_dim(terms_block, values[None, :], slot, 0)]
    pallas_call x0 -> x1, Pallas kernels: none -> 80.8 us  [exchange(): pl.pallas_call(exchange_kernel, out_shape=jax.ShapeDtypeStruct((GX, WIDE)...]
    another operation x1 -> x0, loops' own time: 33.8 us -> none  [shards(): lax.fori_loop(0, pair_total, visit_pair, (empty_terms, empty_terms))]
    mul x15 -> x0, other arithmetic: 33 us -> none  [the longest x7 17.4 us: pair_terms(): distinct[pair_slot] * potential * first_wave]
    dynamic_slice x21 -> x0, local copies, waits for them, and re-layouts: 13.5 us -> none  [the longest x7 4.85 us: visit_pair(): first_row = first_local[pair_slot]]
  transfers between devices with their start and end apart: 4 -> 0, of which waited for: 4 -> 0; matrix products, arithmetic and copies ran while one was open for 1% -> 0% of each run, Pallas kernels for 0% -> 0%
where the time goes in v2:
time: 88.3 us; the launch traced here: 87.5 us
  Pallas kernels  80.8 us (92%)
  local copies, waits for them, and re-layouts  4.36 us (5%)
  other arithmetic  1.66 us (2%)
    pallas_call x1, Pallas kernels, exchange(): pl.pallas_call(exchange_kernel, out_shape=jax.ShapeDtypeStruct((GX, WIDE)...  80.8 us
    unnamed x5, local copies, waits for them, and re-layouts  2.59 us

profile of v2, /device:TPU:8, one launch (start us, length us, event | category | flops | bytes accessed | tf_op | source)
XLA Modules:
  0.0 87.5 jit_solution(8049964810987395778)
XLA Ops:
  0.0 1.7 %reduce = bf16[64000]{0:T(1024)(128)(2,1)S(1)} reduce(bf16[1,64000]{1,0:T(2,128)(2,1)} %param.7, bf16[]{:T(256)} %constant.17), dimensions={0}, to_apply=%param.7.reduce_sub_computation | reduce | bytes 256002 | tf_op args[0]
  1.7 0.2 reshape.6
  1.9 0.2 fusion.3
  2.2 0.1 concatenate.6.own
  2.3 0.8 copy.13.pair_list
  3.7 0.0 copy-start
  3.7 1.1 %copy-done = f32[80,1792]{1,0:T(8,128)S(1)} copy-done((f32[80,1792]{1,0:T(8,128)S(1)}, f32[80,1792]{1,0:T(8,128)}, u32[]{:S(2)}) %copy-start) | copy-done | bytes 573464
  4.7 0.0 copy-start.1
  4.7 0.8 copy-done.1
  5.5 80.8 %exchange.1 = f32[40,1664]{1,0:T(8,128)S(1)} custom-call(bf16[40,1664]{1,0:T(8,128)(2,1)S(1)} %concatenate.6.own, s32[1,8,2]{2,1,0:T(8,128)S(1)} %copy.13.pair_list, s32[1]{0:T(128)S(6)} %copy.22.pair_count, bf16[2,896,896]{2,1,0:T(8,128)(2,1)} %constant.10.clone.plane_high_in, bf16[2,896,896]{2,1,0:T(8,128)(2,1)} %constant.11.clone.plane_low_in, ...), custom_call_target="tpu_custom_call" | custom-call | tf_op jit(solution)/shard_map/exchange/pallas_call | solution.py:522
  86.3 0.1 fusion
  86.4 0.1 concatenate.7
  86.5 1.0 %reshape.7 = f32[1,64000]{1,0:T(1,128)} reshape(f32[40,1600]{1,0:T(8,128)S(1)} %concatenate.7) | data formatting | bytes 512000 | tf_op jit(solution)/shard_map/reshape | solution.py:561
  (5 shorter events, 0.1 us)
Async XLA Ops:
  3.7 1.1 %copy-start = (f32[80,1792]{1,0:T(8,128)S(1)}, f32[80,1792]{1,0:T(8,128)}, u32[]{:S(2)}) copy-start(f32[80,1792]{1,0:T(8,128)} %constant.13.clone.kernel) | copy-start | bytes 1720324
  4.7 0.8 copy-start.1

commit v3 on v2

v3 whole, which is shorter than its diff:
```python
import functools

import jax
import jax.numpy as jnp
import ml_dtypes
import numpy as np
from jax import lax
from jax.experimental import pallas as pl
from jax.experimental.pallas import tpu as pltpu
from jax.sharding import PartitionSpec as P

GX = 40
HALF = GX // 2
PART = HALF * GX
MAIN = 768
TAIL = PART - MAIN
WIDE = 2 * MAIN + 128
FOLD = MAIN + 128
SLOTS = 8
BANDS = 16
NZ, NX = 8, 4
SLAB_ROWS = (16, 16, 8)
SLAB_LANES = (WIDE, WIDE, FOLD)
SLABS = range(3)
screen_width = 0.9
MESH = pl.DeviceIdType.MESH
F32, BF16, I16 = jnp.float32, jnp.bfloat16, jnp.int16
TOP = 32767.0
Z_FIRST = (False, True, False)
ACROSS = False
FAR_ACROSS = False
COPIES = 192
CODED = 22
GREETED = ("z+", "z-", "yh", "x+", "x-", "yl", "core")


def split_np(a):
    high = a.astype(ml_dtypes.bfloat16)
    low = (a - high.astype(np.float64)).astype(ml_dtypes.bfloat16)
    return high, low


@functools.cache
def tables():
    def cas(phase):
        return np.cos(phase) + np.sin(phase)

    n, h = np.arange(GX), np.arange(HALF)
    root = 1.0 / np.sqrt(GX)
    full = cas(2.0 * np.pi * np.outer(n, n) / GX) * root
    even = cas(2.0 * np.pi * np.outer(h, h) / HALF) * root
    odd = cas(2.0 * np.pi * np.outer(2 * h + 1, 2 * h + 1) / (4 * HALF)) * root
    plane = np.zeros((2, FOLD, FOLD))
    plane[0, :PART, :PART] = np.kron(even, full)
    plane[1, :PART, :PART] = np.kron(odd, full)
    plane_high, plane_low = split_np(plane)
    xs = np.concatenate([np.r_[a:b, a:b] for a, b in ((0, 16), (16, 32), (32, 40))])
    pair = np.concatenate([np.r_[[0] * k, [1] * k] for k in (16, 16, 8)])
    both = np.where(pair[:, None] == pair[None, :], full[xs][:, xs], 0.0)
    high, low = split_np(both)
    along = np.concatenate([high, high, low], axis=1)
    signed = np.where(n < GX // 2, n, n - GX) * (2.0 * np.pi / GX)
    squared = signed**2
    total = squared[:, None, None] + squared[None, :, None] + squared[None, None, :]
    safe = np.where(total > 0, total, 1.0)
    screened = 4.0 * np.pi * (1.0 - np.exp(-safe / (4.0 * screen_width**2))) / safe
    kernel = np.where(total > 0, screened, np.pi / screen_width**2)
    padded = np.zeros((GX, 2, FOLD), np.float32)
    padded[:, 0, :PART] = kernel[:, 0::2].reshape(GX, PART)
    padded[:, 1, :PART] = kernel[:, 1::2].reshape(GX, PART)
    sheet = np.zeros((4 * FOLD + 80, FOLD), ml_dtypes.bfloat16)
    sheet[: 2 * FOLD] = plane_high.reshape(2 * FOLD, FOLD)
    sheet[2 * FOLD : 4 * FOLD] = plane_low.reshape(2 * FOLD, FOLD)
    sheet[4 * FOLD :, :240] = along
    return sheet, np.tile(padded.reshape(GX, 2 * FOLD)[xs], (12, 1))


def split(x):
    high = x.astype(BF16)
    return high, (x - high.astype(F32)).astype(BF16)


def encode(value):
    most = jnp.max(jnp.abs(value), axis=1, keepdims=True)
    power = jnp.floor(jnp.log(jnp.maximum(most, 1e-30)) * 1.4426950408889634)
    share = value * (0.5 * jnp.exp2(-power))
    root = share * lax.rsqrt(jnp.maximum(jnp.abs(share), 1e-20))
    code = jnp.clip(jnp.round(root * TOP), -TOP, TOP)
    lanes = lax.broadcasted_iota(jnp.int32, (value.shape[0], 128), 1)
    last = jnp.where(lanes >= 64, power, code[:, -128:])
    return jnp.concatenate([code[:, :-128], last], axis=1).astype(jnp.int32).astype(I16)


def decode(code):
    wide = code.astype(jnp.int32).astype(F32)
    scale = jnp.exp2(wide[:, -64:-63]) * (2.0 / (TOP * TOP))
    return wide * jnp.abs(wide) * scale


def places():
    r, c = lax.axis_index("row"), lax.axis_index("col")
    z, yh = r // 2, r % 2
    x, yl, core = c // 4, (c // 2) % 2, c % 2

    def row_of(dz, y):
        return ((z + dz + NZ) % NZ) * 2 + y

    def col_of(dx, y, k):
        return ((x + dx + NX) % NX) * 4 + y * 2 + k

    ids = {
        "z+": (row_of(1, yh), c),
        "z-": (row_of(-1, yh), c),
        "zf": (row_of(1 - 2 * core, yh), c),
        "zg": (row_of(2 * core - 1, yh), c),
        "zy+": (row_of(1, 1 - yh), c),
        "zy-": (row_of(-1, 1 - yh), c),
        "zyf": (row_of(1 - 2 * core, 1 - yh), c),
        "yh": (row_of(0, 1 - yh), c),
        "x+": (r, col_of(1, yl, core)),
        "x-": (r, col_of(-1, yl, core)),
        "yl": (r, col_of(0, 1 - yl, core)),
        "core": (r, col_of(0, yl, 1 - core)),
    }
    return r, c, yh, yl, core, row_of, col_of, ids


def place_sign(core):
    return 1 - 2 * core


def greet(ids):
    barrier = pltpu.get_barrier_semaphore()
    for where in GREETED:
        pl.semaphore_signal(barrier, inc=1, device_id=ids[where], device_id_type=MESH)


def met():
    pl.semaphore_wait(pltpu.get_barrier_semaphore(), len(GREETED))


class Wires:
    def __init__(self, send_sem, recv_sem, ids):
        self.send_sem, self.recv_sem, self.ids = send_sem, recv_sem, ids
        self.copies, self.waited = {}, set()

    def start(self, name, source, target, where):
        at = len(self.copies)
        copy = pltpu.make_async_remote_copy(
            src_ref=source,
            dst_ref=target,
            send_sem=self.send_sem.at[at],
            recv_sem=self.recv_sem.at[at],
            device_id=self.ids[where],
            device_id_type=MESH,
        )
        copy.start()
        self.copies[name] = copy

    def arrive(self, name):
        if name not in self.waited:
            self.waited.add(name)
            self.copies[name].wait_recv()


RATES = {"z": 1 / 49e3, "x": 1 / 49e3, "y": 1 / 49e3, "l": 1 / 49e3, "c": 1 / 400e3}
DELAYS = {"z": 2.6, "x": 2.6, "y": 3.5, "l": 2.6, "c": 0.7}


class Task:
    def __init__(self, name, needs, cost, body, emits=(), urgent=True):
        self.name, self.needs, self.cost, self.body = name, list(needs), cost, body
        self.emits, self.urgent = list(emits), urgent


def in_order(tasks):
    known, free, left, order, now = {}, {}, list(tasks), [], 0.0
    while left:
        ready = []
        for rank, task in enumerate(left):
            if all(need in known for need in task.needs):
                at = max([known[need] for need in task.needs], default=0.0)
                ready.append((max(at, now), not task.urgent, at, rank))
        at, _, _, rank = min(ready)
        task = left.pop(rank)
        now = at + task.cost
        known[task.name] = now
        for message, link, size in task.emits:
            begin = max(now, *(free.get(part, 0.0) for part in link))
            for part in link:
                free[part] = begin + size * RATES[part[0]]
            known[message] = free[link[0]] + DELAYS[link[0][0]] + 2.0 * (len(link) - 1)
        task.needs.sort(key=known.get)
        order.append(task)
    return order, now


LINKS = {
    "z+": ("z+",), "z-": ("z-",), "zf": ("z+",), "zg": ("z-",), "zy+": ("z+", "y"), "zy-": ("z-", "y"), "zyf": ("z+", "y"),
    "x+": ("x+",), "x-": ("x-",), "yh": ("y",), "yl": ("l",), "core": ("c",),
}


def gather_tasks(wires, place, k, own, cols, rows):
    r, c, yh, yl, core, row_of, col_of, _ = place
    size = 16 * SLAB_LANES[k] * 2
    tasks = []
    messages = []

    def task(name, needs, sends):
        def body():
            for message, where, block, index, source in sends:
                target = block.at[index]
                wires.start(f"{message}{k}", target if source is None else source, target, where)

        emits = [(f"{send[0]}{k}", LINKS[send[1]], size) for send in sends]
        messages.extend(send[0] for send in sends)
        tasks.append(Task(f"gather {name}{k}", [f"{need}{k}" for need in needs], 0.03 * len(sends), body, emits))

    x_first = [("x+a0", "x+", rows, c, own), ("x-a0", "x-", rows, c, own), ("yl", "yl", rows, c, own), ("k0", "core", rows, c, own)]
    if Z_FIRST[k]:
        sign = place_sign(core)
        task("own", [], [("fa0", "zf", cols, r, own), ("ga0", "zg", cols, r, own), ("y0", "yh", cols, r, own), *x_first])
        for way, turn in (("f", -1), ("g", 1)):
            for step in range(3):
                index = row_of(turn * sign * (step + 1), yh)
                sends = [(f"{way}a{step + 1}", "z" + way, cols, index, None)] if step < (3 if way == "f" else 2) else []
                if FAR_ACROSS and way == "f" and step == 2:
                    sends.append(("yf3", "zyf", cols, index, None))
                task(f"{way}{step}", [f"{way}a{step}"], [*sends, (f"y{way}{step}", "yh", cols, index, None)])
        if not FAR_ACROSS:
            task("far", ["fa3"], [("yf3", "yh", cols, row_of(4, yh), None)])
    else:
        beside = [("z+a0", "z+", cols, r, own), ("z-a0", "z-", cols, r, own)]
        across = [("z+b0", "zy+", cols, r, own), ("z-b0", "zy-", cols, r, own)]
        if ACROSS:
            task("own", [], [*beside, *across, *x_first, ("y0", "yh", cols, r, own)])
        else:
            task("own", [], [*beside, ("y0", "yh", cols, r, own), *x_first])
            other = row_of(0, 1 - yh)
            task("y", ["y0"], [("z+b0", "z+", cols, other, None), ("z-b0", "z-", cols, other, None)])
        for where, turn, long in (("z+", -1, "a"), ("z-", 1, "b")):
            for which, y in (("a", yh), ("b", 1 - yh)):
                for step in range(3 if which == long else 2):
                    index = row_of(turn * (step + 1), y)
                    task(f"{where}{which}{step}", [f"{where}{which}{step}"], [(f"{where}{which}{step + 1}", where, cols, index, None)])
    other = col_of(0, 1 - yl, core)
    task("l", ["yl"], [("x+b0", "x+", rows, other, None), ("x-b0", "x-", rows, other, None), ("k1", "core", rows, other, None)])
    for where, turn, long in (("x+", -1, "a"), ("x-", 1, "b")):
        for which, y in (("a", yl), ("b", 1 - yl)):
            index = col_of(turn, y, core)
            sends = [(f"{where}{which}1", where, rows, index, None)] if which == long else []
            task(f"{where}{which}", [f"{where}{which}0"], [*sends, (f"k{where}{which}0", "core", rows, index, None)])
        index = col_of(2, yl if long == "a" else 1 - yl, core)
        task(f"{where}far", [f"{where}{long}1"], [(f"k{where}far", "core", rows, index, None)])
    return tasks, [f"{message}{k}" for message in messages]


def scatter_tasks(wires, place, k, first_at, second_at, firsts, seconds, coded, codes_in, swapped, swaps_in, store):
    r, c, yh, yl, core, row_of, col_of, _ = place
    size = 16 * SLAB_LANES[k] * 2
    weight = SLAB_LANES[k] / WIDE
    tasks, slots = [], {}

    def term(index):
        return seconds[second_at(index)]

    def arrived(message):
        return decode(codes_in[slots[message]])

    def total(value, needs):
        for need in needs:
            value = value + arrived(need)
        return value

    def send(message, where, value, needs, after=()):
        slots[message] = len(slots)

        def body():
            slot = slots[message]
            coded[slot] = encode(total(value(), needs))
            wires.start(f"{message}/{k}", coded.at[slot], codes_in.at[slot], where)

        needed = [f"{need}/{k}" for need in (*needs, *after)] + [f"backward{k}"]
        cost = 0.03 + weight * (0.08 + 0.02 * len(needs))
        tasks.append(Task(f"scatter {message}{k}", needed, cost, body, [(f"{message}/{k}", LINKS[where], size)]))

    def keep(name, value, needs, after=()):
        def body():
            store(total(value(), needs))

        needed = [f"{need}/{k}" for need in (*needs, *after)] + [f"backward{k}"]
        tasks.append(Task(f"keep {name}{k}", needed, 0.04 * weight, body, urgent=False))

    def of(index):
        return functools.partial(term, index)

    order = [(2, "a"), (2, "b"), (1, "b"), (-1, "a"), (1, "a"), (-1, "b"), (0, "b"), (0, "a")]
    y_of = {"a": yl, "b": 1 - yl}

    def swap_all(some):
        def body():
            for slot in some:
                dx, y = order[slot]
                swapped[slot] = firsts[first_at(col_of(dx, y_of[y], 1 - core))]
                wires.start(f"swap{dx}{y}/{k}", swapped.at[slot], swaps_in.at[slot], "core")

        emits = [(f"swap{order[slot][0]}{order[slot][1]}/{k}", LINKS["core"], 2 * size) for slot in some]
        tasks.append(Task(f"swap{some[0]}{k}", [f"backward{k}"], 0.04 * len(some), body, emits))

    def chip_sum(dx, y):
        return firsts[first_at(col_of(dx, y_of[y], core))] + swaps_in[order.index((dx, y))]

    def of_chip(dx, y):
        return functools.partial(chip_sum, dx, y)

    if Z_FIRST[k]:
        sign = place_sign(core)
        spots = {"f3": 4, "f2": 3 * sign, "g2": -3 * sign, "f1": 2 * sign, "g1": -2 * sign, "f0": sign, "g0": -sign, "0": 0}
        if FAR_ACROSS:
            send("pf3", "zf", of(row_of(4, yh)), ())
        for i, (spot, dz) in enumerate(spots.items()):
            send(f"y{spot}", "zyf" if FAR_ACROSS and i == 0 else "yh", of(row_of(dz, 1 - yh)), ())
            if i == 1:
                swap_all(range(0, 4))
            if i == 3:
                swap_all(range(4, 8))
        if not FAR_ACROSS:
            send("pf3", "zf", of(row_of(4, yh)), ("yf3",))
        for spot, needs in (("f2", ("pf3", "yf3") if FAR_ACROSS else ("pf3",)), ("g2", ()), ("f1", ("pf2",)), ("g1", ("pg2",)), ("f0", ("pf1",)), ("g0", ("pg1",))):
            send(f"p{spot}", "z" + spot[0], of(row_of(spots[spot], yh)), (f"y{spot}", *needs))
        keep("z", of(row_of(0, yh)), ("y0", "pf0", "pg0"))
    else:
        y_row = {"a": yh, "b": 1 - yh}

        def chain(where, turn, which, distance, needs):
            way = "zy" + where[1] if ACROSS and which == "b" and distance == 1 else where
            send(f"p{where}{which}{distance}", way, of(row_of(turn * distance, y_row[which])), needs)

        chain("z+", 1, "a", 4, ())
        chain("z-", -1, "b", 4, ())
        swap_all(range(0, 4))
        chain("z+", 1, "b", 3, ())
        chain("z-", -1, "a", 3, ())
        swap_all(range(4, 8))
        for where, turn, long in (("z+", 1, "a"), ("z-", -1, "b")):
            for which in "ab":
                for distance in range(3 if which == long else 2, 0, -1):
                    chain(where, turn, which, distance, (f"p{where}{which}{distance + 1}",))
        direct = ("pz+b1", "pz-b1")
        send("yb", "yh", of(row_of(0, 1 - yh)), () if ACROSS else direct)
        keep("z", of(row_of(0, yh)), ("pz+a1", "pz-a1", "yb", *(direct if ACROSS else ())))
    send("qx+a2", "x+", of_chip(2, "a"), (), ("swap2a",))
    send("qx-b2", "x-", of_chip(2, "b"), (), ("swap2b",))
    send("qx+b1", "x+", of_chip(1, "b"), (), ("swap1b",))
    send("qx-a1", "x-", of_chip(-1, "a"), (), ("swap-1a",))
    send("qx+a1", "x+", of_chip(1, "a"), ("qx+a2",), ("swap1a",))
    send("qx-b1", "x-", of_chip(-1, "b"), ("qx-b2",), ("swap-1b",))
    send("lb", "yl", of_chip(0, "b"), ("qx+b1", "qx-b1"), ("swap0b",))
    keep("x", of_chip(0, "a"), ("qx+a1", "qx-a1", "lb"), ("swap0a",))
    return tasks


def fold(rho, slab):
    rows = SLAB_ROWS[slab]
    if rows == 16:
        near, far, tail = rho[:, :MAIN], rho[:, MAIN : 2 * MAIN], rho[:, 2 * MAIN :]
    else:
        near, far, tail = rho[:rows, :MAIN], rho[rows:, :MAIN], rho[:rows, MAIN:]
    moved = pltpu.roll(tail, 128 - TAIL, 1)
    even = jnp.concatenate([near + far, tail + moved], axis=1)
    return even, jnp.concatenate([near - far, tail - moved], axis=1)


def exchange_kernel(
    own_in, pair_list_in, pair_count_in, sheet_in, kernel_in, out,
    own, pair_list, pair_count, own_0, own_1, own_2, cols_0, cols_1, cols_2, rows_0, rows_1, rows_2,
    dens_0, dens_1, dens_2, spec_0, spec_1, spec_2, first_0, first_1, first_2,
    second_0, second_1, second_2, coded_0, coded_1, coded_2, codes_in_0, codes_in_1, codes_in_2,
    swapped_0, swapped_1, swapped_2, swaps_in_0, swaps_in_1, swaps_in_2,
    kept_0, kept_1, kept_2, sheet, kernel, send_sem, recv_sem, local_sem,
):
    owns, cols, rows = (own_0, own_1, own_2), (cols_0, cols_1, cols_2), (rows_0, rows_1, rows_2)
    dens, spec = (dens_0, dens_1, dens_2), (spec_0, spec_1, spec_2)
    first_sums, second_sums = (first_0, first_1, first_2), (second_0, second_1, second_2)
    coded, codes_in = (coded_0, coded_1, coded_2), (codes_in_0, codes_in_1, codes_in_2)
    kept = (kept_0, kept_1, kept_2)
    swapped, swaps_in = (swapped_0, swapped_1, swapped_2), (swaps_in_0, swaps_in_1, swaps_in_2)
    place = places()
    r, c, ids = place[0], place[1], place[-1]

    local = [
        pltpu.make_async_copy(sheet_in, sheet, local_sem.at[0]),
        pltpu.make_async_copy(kernel_in.at[pl.ds(0, 80)], kernel, local_sem.at[1]),
        pltpu.make_async_copy(pair_list_in, pair_list, local_sem.at[2]),
        pltpu.make_async_copy(pair_count_in, pair_count, local_sem.at[3]),
    ]
    greet(ids)
    take = pltpu.make_async_copy(own_in, own, local_sem.at[10])
    take.start()
    take.wait()
    for k in SLABS:
        size = SLAB_ROWS[k]
        band = own[pl.ds(16 * k, size), :].astype(F32)
        tails = [band[:, MAIN:PART], band[:, PART + MAIN :], jnp.zeros((size, 128 - 2 * TAIL), F32)]
        near, far, tail = band[:, :MAIN], band[:, PART : PART + MAIN], jnp.concatenate(tails, axis=1)
        if size == 16:
            owns[k][...] = jnp.concatenate([near, far, tail], axis=1).astype(BF16)
        else:
            low_rows = jnp.concatenate([far, jnp.zeros((size, 128), F32)], axis=1)
            owns[k][...] = jnp.concatenate([jnp.concatenate([near, tail], axis=1), low_rows], axis=0).astype(BF16)
    met()
    wires = Wires(send_sem, recv_sem, ids)
    keeps = []
    for k in SLABS:
        keeps.append(pltpu.make_async_copy(owns[k], cols[k].at[r], local_sem.at[4 + 2 * k]))
        keeps.append(pltpu.make_async_copy(owns[k], rows[k].at[c], local_sem.at[5 + 2 * k]))

    firsts, seconds, first_band, second_band, before_first, before_second = [], [], [], [], [], []

    def last_slot(bands, wanted):
        at = SLOTS
        for p, band in enumerate(bands):
            at = jnp.where(band == wanted, p, at)
        return at

    def read_pairs():
        count = pair_count[0]
        for p in range(SLOTS):
            first, second = pair_list[0, 0, p], pair_list[0, 1, p]
            other = r * BANDS + first != second * BANDS + c
            firsts.append(first)
            seconds.append(second)
            first_band.append(jnp.where(p < count, first, -1))
            second_band.append(jnp.where((p < count) & other, second, -1))
            before_first.append(last_slot(first_band[:p], first_band[p]))
            before_second.append(last_slot(second_band[:p], second_band[p]))

    def density(k, p):
        return rows[k][firsts[p]].astype(F32) * cols[k][seconds[p]].astype(F32)

    def fill(k, slots):
        size = SLAB_ROWS[k]
        group = 16 // size
        for p in range(slots[0], slots[1], group):
            parts = [fold(density(k, p + i), k) for i in range(group)]
            for parity in range(2):
                value = jnp.concatenate([part[parity] for part in parts], axis=0)
                high, low = split(value)
                dens[k][parity, pl.ds(p * size, 16), :] = high
                dens[k][parity, pl.ds((SLOTS + p) * size, 16), :] = low

    def product(values, parity, at, width):
        lanes = pl.ds(at, width)
        half = values.shape[0] // 2
        wide = jnp.dot(values, sheet[pl.ds(parity * FOLD, FOLD), lanes], preferred_element_type=F32)
        thin = jnp.dot(values[:half], sheet[pl.ds((2 + parity) * FOLD, FOLD), lanes], preferred_element_type=F32)
        return wide[:half] + wide[half:] + thin

    def forward(k, parity, at, width):
        size = SLOTS * SLAB_ROWS[k]
        high, low = split(product(dens[k][parity], parity, at, width))
        lanes = pl.ds(parity * FOLD + at, width)
        spec[k][pl.ds(0, size), lanes] = high
        spec[k][pl.ds(size, size), lanes] = low

    def along():
        return sheet[pl.ds(4 * FOLD, 80), pl.ds(0, 240)]

    def along_x(part):
        high, low = split(part)
        return jnp.dot(along(), jnp.concatenate([high, low, high], axis=0), preferred_element_type=F32)

    def middle(j):
        lanes = pl.ds(j * 256, 256)
        table = kernel[:, lanes]
        for q in range(SLOTS // 2):
            def rows_of(shift):
                return [spec[k][pl.ds((shift * SLOTS + 2 * q) * SLAB_ROWS[k], 2 * SLAB_ROWS[k]), lanes] for k in SLABS]

            high, low = rows_of(0), rows_of(1)
            turned = jnp.dot(along(), jnp.concatenate(high + low + high, axis=0), preferred_element_type=F32)
            high, low = split(along_x(turned * table))
            at = 0
            for k in SLABS:
                size = 2 * SLAB_ROWS[k]
                spec[k][pl.ds(q * size, size), lanes] = high[at : at + size]
                spec[k][pl.ds(SLOTS * SLAB_ROWS[k] + q * size, size), lanes] = low[at : at + size]
                at += size

    def backward(k, at, width):
        size = SLAB_ROWS[k]
        even = product(spec[k][:, pl.ds(0, FOLD)], 0, at, width)
        odd = product(spec[k][:, pl.ds(FOLD, FOLD)], 1, at, width)
        near, far = even + odd, even - odd
        if at == MAIN:
            lane = lax.broadcasted_iota(jnp.int32, near.shape, 1)
            near = jnp.where(lane < TAIL, near, pltpu.roll(far, TAIL, 1))
        for p in range(SLOTS):
            mine = slice(p * size, (p + 1) * size)
            if at == MAIN:
                spans = [(WIDE - 128 if size == 16 else MAIN, near[mine])]
                if size < 16:
                    spans = [(MAIN, jnp.concatenate([near[mine], jnp.zeros_like(near[mine])], axis=0))]
            elif size == 16:
                spans = [(at, near[mine]), (MAIN + at, far[mine])]
            else:
                spans = [(at, jnp.concatenate([near[mine], far[mine]], axis=0))]
            for start, value in spans:
                lanes = pl.ds(start, width)
                to_first = value * cols[k][seconds[p], :, lanes].astype(F32)
                to_second = value * rows[k][firsts[p], :, lanes].astype(F32)
                first_sums[k][p, :, lanes] = to_first + first_sums[k][before_first[p], :, lanes]
                second_sums[k][p, :, lanes] = to_second + second_sums[k][before_second[p], :, lanes]

    stored = set()

    def store(k, value):
        if k not in stored:
            stored.add(k)
            kept[k][...] = value
            return
        value = kept[k][...] + value
        size = SLAB_ROWS[k]
        if size == 16:
            near, far, tail = value[:, :MAIN], value[:, MAIN : 2 * MAIN], value[:, 2 * MAIN :]
        else:
            near, far, tail = value[:size, :MAIN], value[size:, :MAIN], value[:size, MAIN:]
        out[pl.ds(16 * k, size), :] = jnp.concatenate([near, tail[:, :TAIL], far, tail[:, TAIL : 2 * TAIL]], axis=1)

    def begin():
        for copy in local:
            copy.start()
        for copy in keeps:
            copy.start()

    def clear():
        for k in SLABS:
            first_sums[k][SLOTS] = jnp.zeros(first_sums[k].shape[1:], F32)
            second_sums[k][SLOTS] = jnp.zeros(second_sums[k].shape[1:], F32)
        for copy in (*local, *keeps):
            copy.wait()
        read_pairs()

    def nothing():
        pass

    tasks, filled = [], []
    for k in SLABS:
        some, messages = gather_tasks(wires, place, k, owns[k], cols[k], rows[k])
        tasks += some
        filled.append(messages)
    tasks.append(Task("begin", [], 0.1, begin))
    tasks.append(Task("clear", ["begin", "z+a10"], 0.5, clear, urgent=False))

    def piece(name, needs, cost, body):
        tasks.append(Task(name, needs, cost, body, urgent=False))

    turned = []
    for k in SLABS:
        weight = SLAB_LANES[k] / WIDE
        for half in range(2):
            piece(f"fill{k}{half}", [*filled[k], "clear"], 0.25 * weight, functools.partial(fill, k, (4 * half, 4 * half + 4)))
        for parity in range(2):
            for at, width in ((0, 512), (512, 384)):
                name = f"forward{k}{parity}{at}"
                turned.append(name)
                piece(name, [f"fill{k}0", f"fill{k}1"], 0.35 * weight, functools.partial(forward, k, parity, at, width))
    def all_middle():
        for j in range(2 * FOLD // 256):
            middle(j)

    piece("middle", turned, 2.5, all_middle)
    for k in SLABS:
        weight = SLAB_LANES[k] / WIDE
        before, names = ["middle"], []
        for at, width in ((0, 256), (256, 256), (512, 256), (768, 128)):
            names.append(f"backward{k}{at}")
            piece(names[-1], before, width / 256 * 0.6 * weight, functools.partial(backward, k, at, width))
        piece(f"backward{k}", names, 0.0, nothing)
        tasks[-1].urgent = True
        tasks += scatter_tasks(
            wires, place, k, functools.partial(last_slot, first_band), functools.partial(last_slot, second_band),
            first_sums[k], second_sums[k], coded[k], codes_in[k], swapped[k], swaps_in[k],
            functools.partial(store, k),
        )
    for task in in_order(tasks)[0]:
        for need in task.needs:
            if need in wires.copies:
                wires.arrive(need)
        task.body()
    for copy in wires.copies.values():
        copy.wait_send()


def exchange(own, pair_list, pair_count):
    vmem = pl.BlockSpec(memory_space=pltpu.VMEM)
    anywhere = pl.BlockSpec(memory_space=pl.ANY)
    sheet, kernel = (jnp.asarray(t) for t in tables())

    def each(shape, kind):
        return [pltpu.VMEM(shape(k), kind) for k in SLABS]

    def stack(count):
        return lambda k: (count, 16, SLAB_LANES[k])

    return pl.pallas_call(
        exchange_kernel,
        out_shape=jax.ShapeDtypeStruct((GX, GX * GX), F32),
        in_specs=[anywhere] * 5,
        out_specs=vmem,
        scratch_shapes=[
            pltpu.VMEM(own.shape, BF16),
            pltpu.SMEM(pair_list.shape, jnp.int32),
            pltpu.SMEM(pair_count.shape, jnp.int32),
            *each(lambda k: (16, SLAB_LANES[k]), BF16),
            *each(stack(BANDS), BF16),
            *each(stack(BANDS), BF16),
            *each(lambda k: (2, 2 * SLOTS * SLAB_ROWS[k], FOLD), BF16),
            *each(lambda k: (2 * SLOTS * SLAB_ROWS[k], 2 * FOLD), BF16),
            *each(stack(SLOTS + 1), F32),
            *each(stack(SLOTS + 1), F32),
            *each(stack(CODED), I16),
            *each(stack(CODED), I16),
            *each(stack(SLOTS), F32),
            *each(stack(SLOTS), F32),
            *each(lambda k: (16, SLAB_LANES[k]), F32),
            pltpu.VMEM(sheet.shape, BF16),
            pltpu.VMEM((80, 2 * FOLD), F32),
            pltpu.SemaphoreType.DMA((COPIES,)),
            pltpu.SemaphoreType.DMA((COPIES,)),
            pltpu.SemaphoreType.DMA((11,)),
        ],
        compiler_params=pltpu.CompilerParams(
            collective_id=0, has_side_effects=True, vmem_limit_bytes=58 * 1024 * 1024
        ),
        name="exchange",
    )(own, pair_list, pair_count, sheet, kernel)


def shards(orbitals, pair_list, pair_count):
    fields = exchange(orbitals.reshape(GX, GX * GX), jnp.swapaxes(pair_list, 1, 2), pair_count)
    return fields.reshape(1, GX * GX * GX)


def solution(mesh):
    return jax.shard_map(
        shards,
        mesh=mesh,
        in_specs=(P(("row", "col"), None), P(("row", "col"), None, None), P(("row", "col"))),
        out_specs=P(("row", "col"), None),
        check_vma=False,
    )
```

time: 88.3 us -> 75.2 us (0.85)
  Pallas kernels: 80.8 us -> 69.2 us
  local copies, waits for them, and re-layouts: 4.36 us -> 2.75 us
    pallas_call x1, Pallas kernels: 80.8 us -> 69.2 us  [exchange(): pl.pallas_call(exchange_kernel, out_shape=jax.ShapeDtypeStruct((GX, GX *...]
    unnamed x5 -> x0, local copies, waits for them, and re-layouts: 2.59 us -> none
    reshape x2, local copies, waits for them, and re-layouts: 1.23 us -> 2.75 us  [the longest x1 1.94 us: shards(): return fields.reshape(1, GX * GX * GX)]
where the time goes in v3:
time: 75.2 us; the launch traced here: 74.3 us
  Pallas kernels  69.2 us (92%)
  local copies, waits for them, and re-layouts  2.75 us (4%)
  other arithmetic  1.66 us (2%)
    pallas_call x1, Pallas kernels, exchange(): pl.pallas_call(exchange_kernel, out_shape=jax.ShapeDtypeStruct((GX, GX *...  69.2 us
    reshape x1, local copies, waits for them, and re-layouts, shards(): return fields.reshape(1, GX * GX * GX)  1.94 us
    unnamed x1, other arithmetic  1.66 us

profile of v3, /device:TPU:8, one launch (start us, length us, event | category | flops | bytes accessed | tf_op | source)
XLA Modules:
  0.0 74.3 jit_solution(6237883372922961735)
XLA Ops:
  0.7 1.7 %reduce = bf16[64000]{0:T(1024)(128)(2,1)S(1)} reduce(bf16[1,64000]{1,0:T(2,128)(2,1)} %param.5, bf16[]{:T(256)} %constant.9), dimensions={0}, to_apply=%param.5.reduce_sub_computation | reduce | bytes 256002 | tf_op args[0]
  2.3 0.8 %reshape.6.own_in = bf16[40,1600]{1,0:T(8,128)(2,1)} reshape(bf16[64000]{0:T(1024)(128)(2,1)S(1)} %reduce) | data formatting | bytes 256000 | tf_op jit(solution)/shard_map/reshape | solution.py:642
  3.1 69.2 %exchange.1 = f32[40,1600]{1,0:T(8,128)} custom-call(bf16[40,1600]{1,0:T(8,128)(2,1)} %reshape.6.own_in, s32[1,2,8]{2,1,0:T(2,128)} %bitcast.1, s32[1]{0:T(128)S(6)} %copy.6.pair_count_in, bf16[3664,896]{1,0:T(8,128)(2,1)} %constant.4.clone.sheet_in, f32[960,1792]{1,0:T(8,128)} %constant.5.clone.kernel_in), custom_call_target="tpu_custom_call" | custom-call | tf_op jit(solution)/shard_map/exchange/pallas_call | solution.py:607
  72.4 1.9 %reshape.7 = f32[1,64000]{1,0:T(1,128)} reshape(f32[40,1600]{1,0:T(8,128)} %exchange.1) | data formatting | bytes 512000 | tf_op jit(solution)/shard_map/reshape | solution.py:643

commit v4 on v3

--- a/solution.py
+++ b/solution.py
@@ -26,12 +26,13 @@
 MESH = pl.DeviceIdType.MESH
 F32, BF16, I16 = jnp.float32, jnp.bfloat16, jnp.int16
 TOP = 32767.0
-Z_FIRST = (False, True, False)
-ACROSS = False
-FAR_ACROSS = False
+Z_FIRST = (True, False, False)
+FAR = (True, False, False)
+GATHER_ORDER = (0, 1, 2)
+SCATTER_ORDER = (2, 1, 0)
 COPIES = 192
 CODED = 22
-GREETED = ("z+", "z-", "yh", "x+", "x-", "yl", "core")
+GREETED = ("z+", "z-", "zz+", "zz-", "yh", "x+", "x-", "yl", "core")
 
 
 def split_np(a):
@@ -113,9 +114,9 @@
         "z-": (row_of(-1, yh), c),
         "zf": (row_of(1 - 2 * core, yh), c),
         "zg": (row_of(2 * core - 1, yh), c),
-        "zy+": (row_of(1, 1 - yh), c),
-        "zy-": (row_of(-1, 1 - yh), c),
-        "zyf": (row_of(1 - 2 * core, 1 - yh), c),
+        "zz+": (row_of(2, yh), c),
+        "zz-": (row_of(-2, yh), c),
+        "zzf": (row_of(2 - 4 * core, yh), c),
         "yh": (row_of(0, 1 - yh), c),
         "x+": (r, col_of(1, yl, core)),
         "x-": (r, col_of(-1, yl, core)),
@@ -164,40 +165,40 @@
 
 
 RATES = {"z": 1 / 49e3, "x": 1 / 49e3, "y": 1 / 49e3, "l": 1 / 49e3, "c": 1 / 400e3}
-DELAYS = {"z": 2.6, "x": 2.6, "y": 3.5, "l": 2.6, "c": 0.7}
+DELAYS = {"z": 2.9, "x": 2.9, "y": 3.2, "l": 2.9, "c": 0.7}
 
 
 class Task:
-    def __init__(self, name, needs, cost, body, emits=(), urgent=True):
+    def __init__(self, name, needs, cost, body, emits=(), rank=0):
         self.name, self.needs, self.cost, self.body = name, list(needs), cost, body
-        self.emits, self.urgent = list(emits), urgent
+        self.emits, self.rank = list(emits), rank
 
 
 def in_order(tasks):
     known, free, left, order, now = {}, {}, list(tasks), [], 0.0
     while left:
         ready = []
-        for rank, task in enumerate(left):
+        for i, task in enumerate(left):
             if all(need in known for need in task.needs):
                 at = max([known[need] for need in task.needs], default=0.0)
-                ready.append((max(at, now), not task.urgent, at, rank))
-        at, _, _, rank = min(ready)
-        task = left.pop(rank)
+                ready.append((max(at, now), task.rank, at, i))
+        at, _, _, i = min(ready)
+        task = left.pop(i)
         now = at + task.cost
         known[task.name] = now
-        for message, link, size in task.emits:
-            begin = max(now, *(free.get(part, 0.0) for part in link))
-            for part in link:
-                free[part] = begin + size * RATES[part[0]]
-            known[message] = free[link[0]] + DELAYS[link[0][0]] + 2.0 * (len(link) - 1)
+        for message, (link, hops), size in task.emits:
+            time = size * RATES[link[0]]
+            begin = max(now, free.get(link, 0.0))
+            free[link] = begin + time * hops
+            known[message] = begin + time + DELAYS[link[0]] + 1.0 * (hops - 1)
         task.needs.sort(key=known.get)
         order.append(task)
     return order, now
 
 
 LINKS = {
-    "z+": ("z+",), "z-": ("z-",), "zf": ("z+",), "zg": ("z-",), "zy+": ("z+", "y"), "zy-": ("z-", "y"), "zyf": ("z+", "y"),
-    "x+": ("x+",), "x-": ("x-",), "yh": ("y",), "yl": ("l",), "core": ("c",),
+    "z+": ("z+", 1), "z-": ("z-", 1), "zf": ("z+", 1), "zg": ("z-", 1), "zz+": ("z+", 2), "zz-": ("z-", 2), "zzf": ("z+", 2),
+    "x+": ("x+", 1), "x-": ("x-", 1), "yh": ("y", 1), "yl": ("l", 1), "core": ("c", 1),
 }
 
 
@@ -224,26 +225,24 @@
         for way, turn in (("f", -1), ("g", 1)):
             for step in range(3):
                 index = row_of(turn * sign * (step + 1), yh)
-                sends = [(f"{way}a{step + 1}", "z" + way, cols, index, None)] if step < (3 if way == "f" else 2) else []
-                if FAR_ACROSS and way == "f" and step == 2:
-                    sends.append(("yf3", "zyf", cols, index, None))
+                sends = [(f"{way}a{step + 1}", "z" + way, cols, index, None)] if step < 2 else []
+                if way == "f" and step == (1 if FAR[k] else 2):
+                    sends.append(("fa3", "zzf" if FAR[k] else "zf", cols, index, None))
                 task(f"{way}{step}", [f"{way}a{step}"], [*sends, (f"y{way}{step}", "yh", cols, index, None)])
-        if not FAR_ACROSS:
-            task("far", ["fa3"], [("yf3", "yh", cols, row_of(4, yh), None)])
+        task("far", ["fa3"], [("yf3", "yh", cols, row_of(4, yh), None)])
     else:
         beside = [("z+a0", "z+", cols, r, own), ("z-a0", "z-", cols, r, own)]
-        across = [("z+b0", "zy+", cols, r, own), ("z-b0", "zy-", cols, r, own)]
-        if ACROSS:
-            task("own", [], [*beside, *across, *x_first, ("y0", "yh", cols, r, own)])
-        else:
-            task("own", [], [*beside, ("y0", "yh", cols, r, own), *x_first])
-            other = row_of(0, 1 - yh)
-            task("y", ["y0"], [("z+b0", "z+", cols, other, None), ("z-b0", "z-", cols, other, None)])
+        task("own", [], [*beside, ("y0", "yh", cols, r, own), *x_first])
+        other = row_of(0, 1 - yh)
+        task("y", ["y0"], [("z+b0", "z+", cols, other, None), ("z-b0", "z-", cols, other, None)])
         for where, turn, long in (("z+", -1, "a"), ("z-", 1, "b")):
             for which, y in (("a", yh), ("b", 1 - yh)):
-                for step in range(3 if which == long else 2):
+                for step in range(3 if which == long and not FAR[k] else 2):
                     index = row_of(turn * (step + 1), y)
-                    task(f"{where}{which}{step}", [f"{where}{which}{step}"], [(f"{where}{which}{step + 1}", where, cols, index, None)])
+                    sends = [(f"{where}{which}{step + 1}", where, cols, index, None)]
+                    if which == long and FAR[k] and step == 1:
+                        sends.append((f"{where}{which}3", "z" + where, cols, index, None))
+                    task(f"{where}{which}{step}", [f"{where}{which}{step}"], sends)
     other = col_of(0, 1 - yl, core)
     task("l", ["yl"], [("x+b0", "x+", rows, other, None), ("x-b0", "x-", rows, other, None), ("k1", "core", rows, other, None)])
     for where, turn, long in (("x+", -1, "a"), ("x-", 1, "b")):
@@ -273,7 +272,7 @@
             value = value + arrived(need)
         return value
 
-    def send(message, where, value, needs, after=()):
+    def send(message, where, value, needs, after=(), rank=0):
         slots[message] = len(slots)
 
         def body():
@@ -283,14 +282,14 @@
 
         needed = [f"{need}/{k}" for need in (*needs, *after)] + [f"backward{k}"]
         cost = 0.03 + weight * (0.08 + 0.02 * len(needs))
-        tasks.append(Task(f"scatter {message}{k}", needed, cost, body, [(f"{message}/{k}", LINKS[where], size)]))
+        tasks.append(Task(f"scatter {message}{k}", needed, cost, body, [(f"{message}/{k}", LINKS[where], size)], rank))
 
     def keep(name, value, needs, after=()):
         def body():
             store(total(value(), needs))
 
         needed = [f"{need}/{k}" for need in (*needs, *after)] + [f"backward{k}"]
-        tasks.append(Task(f"keep {name}{k}", needed, 0.04 * weight, body, urgent=False))
+        tasks.append(Task(f"keep {name}{k}", needed, 0.04 * weight, body, rank=2))
 
     def of(index):
         return functools.partial(term, index)
@@ -306,7 +305,7 @@
                 wires.start(f"swap{dx}{y}/{k}", swapped.at[slot], swaps_in.at[slot], "core")
 
         emits = [(f"swap{order[slot][0]}{order[slot][1]}/{k}", LINKS["core"], 2 * size) for slot in some]
-        tasks.append(Task(f"swap{some[0]}{k}", [f"backward{k}"], 0.04 * len(some), body, emits))
+        tasks.append(Task(f"swap{some[0]}{k}", [f"backward{k}"], 0.04 * len(some), body, emits, rank=2))
 
     def chip_sum(dx, y):
         return firsts[first_at(col_of(dx, y_of[y], core))] + swaps_in[order.index((dx, y))]
@@ -317,24 +316,23 @@
     if Z_FIRST[k]:
         sign = place_sign(core)
         spots = {"f3": 4, "f2": 3 * sign, "g2": -3 * sign, "f1": 2 * sign, "g1": -2 * sign, "f0": sign, "g0": -sign, "0": 0}
-        if FAR_ACROSS:
-            send("pf3", "zf", of(row_of(4, yh)), ())
         for i, (spot, dz) in enumerate(spots.items()):
-            send(f"y{spot}", "zyf" if FAR_ACROSS and i == 0 else "yh", of(row_of(dz, 1 - yh)), ())
+            send(f"y{spot}", "yh", of(row_of(dz, 1 - yh)), ())
             if i == 1:
                 swap_all(range(0, 4))
             if i == 3:
                 swap_all(range(4, 8))
-        if not FAR_ACROSS:
-            send("pf3", "zf", of(row_of(4, yh)), ("yf3",))
-        for spot, needs in (("f2", ("pf3", "yf3") if FAR_ACROSS else ("pf3",)), ("g2", ()), ("f1", ("pf2",)), ("g1", ("pg2",)), ("f0", ("pf1",)), ("g0", ("pg1",))):
-            send(f"p{spot}", "z" + spot[0], of(row_of(spots[spot], yh)), (f"y{spot}", *needs))
+        before = {"f3": (), "f2": () if FAR[k] else ("pf3",), "g2": (), "f1": ("pf2", "pf3") if FAR[k] else ("pf2",)}
+        before |= {"g1": ("pg2",), "f0": ("pf1",), "g0": ("pg1",)}
+        for spot, needs in before.items():
+            where = "zzf" if FAR[k] and spot == "f3" else "z" + spot[0]
+            send(f"p{spot}", where, of(row_of(spots[spot], yh)), (f"y{spot}", *needs))
         keep("z", of(row_of(0, yh)), ("y0", "pf0", "pg0"))
     else:
         y_row = {"a": yh, "b": 1 - yh}
 
         def chain(where, turn, which, distance, needs):
-            way = "zy" + where[1] if ACROSS and which == "b" and distance == 1 else where
+            way = "z" + where if FAR[k] and distance == 4 else where
             send(f"p{where}{which}{distance}", way, of(row_of(turn * distance, y_row[which])), needs)
 
         chain("z+", 1, "a", 4, ())
@@ -346,17 +344,19 @@
         for where, turn, long in (("z+", 1, "a"), ("z-", -1, "b")):
             for which in "ab":
                 for distance in range(3 if which == long else 2, 0, -1):
-                    chain(where, turn, which, distance, (f"p{where}{which}{distance + 1}",))
-        direct = ("pz+b1", "pz-b1")
-        send("yb", "yh", of(row_of(0, 1 - yh)), () if ACROSS else direct)
-        keep("z", of(row_of(0, yh)), ("pz+a1", "pz-a1", "yb", *(direct if ACROSS else ())))
-    send("qx+a2", "x+", of_chip(2, "a"), (), ("swap2a",))
-    send("qx-b2", "x-", of_chip(2, "b"), (), ("swap2b",))
-    send("qx+b1", "x+", of_chip(1, "b"), (), ("swap1b",))
-    send("qx-a1", "x-", of_chip(-1, "a"), (), ("swap-1a",))
-    send("qx+a1", "x+", of_chip(1, "a"), ("qx+a2",), ("swap1a",))
-    send("qx-b1", "x-", of_chip(-1, "b"), ("qx-b2",), ("swap-1b",))
-    send("lb", "yl", of_chip(0, "b"), ("qx+b1", "qx-b1"), ("swap0b",))
+                    needs = [f"p{where}{which}{distance + 1}"]
+                    if which == long and FAR[k]:
+                        needs = [] if distance == 3 else [*needs, f"p{where}{which}4"] if distance == 2 else needs
+                    chain(where, turn, which, distance, needs)
+        send("yb", "yh", of(row_of(0, 1 - yh)), ("pz+b1", "pz-b1"))
+        keep("z", of(row_of(0, yh)), ("pz+a1", "pz-a1", "yb"))
+    send("qx+a2", "x+", of_chip(2, "a"), (), ("swap2a",), 2)
+    send("qx-b2", "x-", of_chip(2, "b"), (), ("swap2b",), 2)
+    send("qx+b1", "x+", of_chip(1, "b"), (), ("swap1b",), 2)
+    send("qx-a1", "x-", of_chip(-1, "a"), (), ("swap-1a",), 2)
+    send("qx+a1", "x+", of_chip(1, "a"), ("qx+a2",), ("swap1a",), 2)
+    send("qx-b1", "x-", of_chip(-1, "b"), ("qx-b2",), ("swap-1b",), 2)
+    send("lb", "yl", of_chip(0, "b"), ("qx+b1", "qx-b1"), ("swap0b",), 2)
     keep("x", of_chip(0, "a"), ("qx+a1", "qx-a1", "lb"), ("swap0a",))
     return tasks
 
@@ -545,19 +545,19 @@
     def nothing():
         pass
 
-    tasks, filled = [], []
-    for k in SLABS:
+    tasks, filled = [], {}
+    for k in GATHER_ORDER:
         some, messages = gather_tasks(wires, place, k, owns[k], cols[k], rows[k])
         tasks += some
-        filled.append(messages)
+        filled[k] = messages
     tasks.append(Task("begin", [], 0.1, begin))
-    tasks.append(Task("clear", ["begin", "z+a10"], 0.5, clear, urgent=False))
+    tasks.append(Task("clear", ["begin", "fa10" if Z_FIRST[0] else "z+a10"], 0.5, clear, rank=1))
 
     def piece(name, needs, cost, body):
-        tasks.append(Task(name, needs, cost, body, urgent=False))
+        tasks.append(Task(name, needs, cost, body, rank=1))
 
     turned = []
-    for k in SLABS:
+    for k in GATHER_ORDER:
         weight = SLAB_LANES[k] / WIDE
         for half in range(2):
             piece(f"fill{k}{half}", [*filled[k], "clear"], 0.25 * weight, functools.partial(fill, k, (4 * half, 4 * half + 4)))
@@ -565,20 +565,20 @@
             for at, width in ((0, 512), (512, 384)):
                 name = f"forward{k}{parity}{at}"
                 turned.append(name)
-                piece(name, [f"fill{k}0", f"fill{k}1"], 0.35 * weight, functools.partial(forward, k, parity, at, width))
+                piece(name, [f"fill{k}0", f"fill{k}1"], 0.3 * weight, functools.partial(forward, k, parity, at, width))
     def all_middle():
         for j in range(2 * FOLD // 256):
             middle(j)
 
     piece("middle", turned, 2.5, all_middle)
-    for k in SLABS:
+    for k in SCATTER_ORDER:
         weight = SLAB_LANES[k] / WIDE
         before, names = ["middle"], []
         for at, width in ((0, 256), (256, 256), (512, 256), (768, 128)):
             names.append(f"backward{k}{at}")
             piece(names[-1], before, width / 256 * 0.6 * weight, functools.partial(backward, k, at, width))
         piece(f"backward{k}", names, 0.0, nothing)
-        tasks[-1].urgent = True
+        tasks[-1].rank = 0
         tasks += scatter_tasks(
             wires, place, k, functools.partial(last_slot, first_band), functools.partial(last_slot, second_band),
             first_sums[k], second_sums[k], coded[k], codes_in[k], swapped[k], swaps_in[k],

time: 75.2 us -> 71.8 us (0.955)
  Pallas kernels: 69.2 us -> 65.9 us
    pallas_call x1, Pallas kernels: 69.2 us -> 65.9 us  [exchange(): pl.pallas_call(exchange_kernel, out_shape=jax.ShapeDtypeStruct((GX, GX *...]
where the time goes in v4:
time: 71.8 us; the launch traced here: 71 us
  Pallas kernels  65.9 us (92%)
  local copies, waits for them, and re-layouts  2.75 us (4%)
  other arithmetic  1.66 us (2%)
    pallas_call x1, Pallas kernels, exchange(): pl.pallas_call(exchange_kernel, out_shape=jax.ShapeDtypeStruct((GX, GX *...  65.9 us
    reshape x1, local copies, waits for them, and re-layouts, shards(): return fields.reshape(1, GX * GX * GX)  1.94 us
    unnamed x1, other arithmetic  1.66 us

profile of v4, /device:TPU:8, one launch (start us, length us, event | category | flops | bytes accessed | tf_op | source)
XLA Modules:
  0.0 71.0 jit_solution(17520000523337350509)
XLA Ops:
  0.7 1.7 %reduce = bf16[64000]{0:T(1024)(128)(2,1)S(1)} reduce(bf16[1,64000]{1,0:T(2,128)(2,1)} %param.5, bf16[]{:T(256)} %constant.9), dimensions={0}, to_apply=%param.5.reduce_sub_computation | reduce | bytes 256002 | tf_op args[0]
  2.3 0.8 %reshape.6.own_in = bf16[40,1600]{1,0:T(8,128)(2,1)} reshape(bf16[64000]{0:T(1024)(128)(2,1)S(1)} %reduce) | data formatting | bytes 256000 | tf_op jit(solution)/shard_map/reshape | solution.py:642
  3.1 65.9 %exchange.1 = f32[40,1600]{1,0:T(8,128)} custom-call(bf16[40,1600]{1,0:T(8,128)(2,1)} %reshape.6.own_in, s32[1,2,8]{2,1,0:T(2,128)} %bitcast.1, s32[1]{0:T(128)S(6)} %copy.6.pair_count_in, bf16[3664,896]{1,0:T(8,128)(2,1)} %constant.4.clone.sheet_in, f32[960,1792]{1,0:T(8,128)} %constant.5.clone.kernel_in), custom_call_target="tpu_custom_call" | custom-call | tf_op jit(solution)/shard_map/exchange/pallas_call | solution.py:607
  69.1 1.9 %reshape.7 = f32[1,64000]{1,0:T(1,128)} reshape(f32[40,1600]{1,0:T(8,128)} %exchange.1) | data formatting | bytes 512000 | tf_op jit(solution)/shard_map/reshape | solution.py:643

commit v5 on v4

--- a/solution.py
+++ b/solution.py
@@ -28,8 +28,8 @@
 TOP = 32767.0
 Z_FIRST = (True, False, False)
 FAR = (True, False, False)
-GATHER_ORDER = (0, 1, 2)
-SCATTER_ORDER = (2, 1, 0)
+GATHER_ORDER = (2, 0, 1)
+SCATTER_ORDER = (1, 2, 0)
 COPIES = 192
 CODED = 22
 GREETED = ("z+", "z-", "zz+", "zz-", "yh", "x+", "x-", "yl", "core")
@@ -73,7 +73,7 @@
     sheet[: 2 * FOLD] = plane_high.reshape(2 * FOLD, FOLD)
     sheet[2 * FOLD : 4 * FOLD] = plane_low.reshape(2 * FOLD, FOLD)
     sheet[4 * FOLD :, :240] = along
-    return sheet, np.tile(padded.reshape(GX, 2 * FOLD)[xs], (12, 1))
+    return sheet, padded.reshape(GX, 2 * FOLD)[xs]
 
 
 def split(x):
@@ -221,7 +221,8 @@
     x_first = [("x+a0", "x+", rows, c, own), ("x-a0", "x-", rows, c, own), ("yl", "yl", rows, c, own), ("k0", "core", rows, c, own)]
     if Z_FIRST[k]:
         sign = place_sign(core)
-        task("own", [], [("fa0", "zf", cols, r, own), ("ga0", "zg", cols, r, own), ("y0", "yh", cols, r, own), *x_first])
+        task("own", [], [("fa0", "zf", cols, r, own), ("ga0", "zg", cols, r, own), *x_first])
+        task("own y", ["fa0"], [("y0", "yh", cols, r, own)])
         for way, turn in (("f", -1), ("g", 1)):
             for step in range(3):
                 index = row_of(turn * sign * (step + 1), yh)
@@ -391,7 +392,7 @@
 
     local = [
         pltpu.make_async_copy(sheet_in, sheet, local_sem.at[0]),
-        pltpu.make_async_copy(kernel_in.at[pl.ds(0, 80)], kernel, local_sem.at[1]),
+        pltpu.make_async_copy(kernel_in, kernel, local_sem.at[1]),
         pltpu.make_async_copy(pair_list_in, pair_list, local_sem.at[2]),
         pltpu.make_async_copy(pair_count_in, pair_count, local_sem.at[3]),
     ]
@@ -399,9 +400,14 @@
     take = pltpu.make_async_copy(own_in, own, local_sem.at[10])
     take.start()
     take.wait()
+    def own_row(x):
+        skipped = GX * GX * x % 128
+        line = own[:, pl.ds(GX * GX * x - skipped, WIDE)].astype(F32)
+        return line[:, skipped : skipped + GX * GX]
+
     for k in SLABS:
         size = SLAB_ROWS[k]
-        band = own[pl.ds(16 * k, size), :].astype(F32)
+        band = jnp.concatenate([own_row(x) for x in range(16 * k, 16 * k + size)], axis=0)
         tails = [band[:, MAIN:PART], band[:, PART + MAIN :], jnp.zeros((size, 128 - 2 * TAIL), F32)]
         near, far, tail = band[:, :MAIN], band[:, PART : PART + MAIN], jnp.concatenate(tails, axis=1)
         if size == 16:
@@ -595,7 +601,7 @@
 
 def exchange(own, pair_list, pair_count):
     vmem = pl.BlockSpec(memory_space=pltpu.VMEM)
-    anywhere = pl.BlockSpec(memory_space=pl.ANY)
+    hbm = pl.BlockSpec(memory_space=pltpu.HBM)
     sheet, kernel = (jnp.asarray(t) for t in tables())
 
     def each(shape, kind):
@@ -607,7 +613,7 @@
     return pl.pallas_call(
         exchange_kernel,
         out_shape=jax.ShapeDtypeStruct((GX, GX * GX), F32),
-        in_specs=[anywhere] * 5,
+        in_specs=[hbm] * 5,
         out_specs=vmem,
         scratch_shapes=[
             pltpu.VMEM(own.shape, BF16),
@@ -626,20 +632,20 @@
             *each(stack(SLOTS), F32),
             *each(lambda k: (16, SLAB_LANES[k]), F32),
             pltpu.VMEM(sheet.shape, BF16),
-            pltpu.VMEM((80, 2 * FOLD), F32),
+            pltpu.VMEM(kernel.shape, F32),
             pltpu.SemaphoreType.DMA((COPIES,)),
             pltpu.SemaphoreType.DMA((COPIES,)),
             pltpu.SemaphoreType.DMA((11,)),
         ],
         compiler_params=pltpu.CompilerParams(
-            collective_id=0, has_side_effects=True, vmem_limit_bytes=58 * 1024 * 1024
+            collective_id=0, has_side_effects=True, vmem_limit_bytes=62 * 1024 * 1024
         ),
         name="exchange",
     )(own, pair_list, pair_count, sheet, kernel)
 
 
 def shards(orbitals, pair_list, pair_count):
-    fields = exchange(orbitals.reshape(GX, GX * GX), jnp.swapaxes(pair_list, 1, 2), pair_count)
+    fields = exchange(orbitals, jnp.swapaxes(pair_list, 1, 2), pair_count)
     return fields.reshape(1, GX * GX * GX)
 
 

time: 71.8 us -> 68.6 us (0.955)
  other arithmetic: 1.66 us -> 0 us
  local copies, waits for them, and re-layouts: 2.75 us -> 1.94 us
    unnamed x1 -> x0, other arithmetic: 1.66 us -> none
    reshape x1 -> x0, local copies, waits for them, and re-layouts: 0.81 us -> none  [shards(): orbitals.reshape(GX, GX * GX)]
where the time goes in v5:
time: 68.6 us; the launch traced here: 68.4 us
  Pallas kernels  65.8 us (96%)
  local copies, waits for them, and re-layouts  1.94 us (3%)
    pallas_call x1, Pallas kernels, exchange(): pl.pallas_call(exchange_kernel, out_shape=jax.ShapeDtypeStruct((GX, GX *...  65.8 us
    reshape x1, local copies, waits for them, and re-layouts, shards(): return fields.reshape(1, GX * GX * GX)  1.94 us

profile of v5, /device:TPU:8, one launch (start us, length us, event | category | flops | bytes accessed | tf_op | source)
XLA Modules:
  0.0 68.4 jit_solution(13168087066641984106)
XLA Ops:
  0.7 65.8 %exchange.1 = f32[40,1600]{1,0:T(8,128)} custom-call(bf16[1,64000]{1,0:T(2,128)(2,1)} %own_in.1, s32[1,2,8]{2,1,0:T(2,128)} %bitcast.1, s32[1]{0:T(128)S(6)} %copy.6.pair_count_in, bf16[3664,896]{1,0:T(8,128)(2,1)} %constant.4.clone.sheet_in, f32[80,1792]{1,0:T(8,128)} %constant.5.clone.kernel_in), custom_call_target="tpu_custom_call" | custom-call | tf_op jit(solution)/shard_map/exchange/pallas_call | solution.py:613
  66.4 1.9 %reshape.3 = f32[1,64000]{1,0:T(1,128)} reshape(f32[40,1600]{1,0:T(8,128)} %exchange.1) | data formatting | bytes 512000 | tf_op jit(solution)/shard_map/reshape | solution.py:649

commit v6 on v5

--- a/solution.py
+++ b/solution.py
@@ -30,6 +30,8 @@
 FAR = (True, False, False)
 GATHER_ORDER = (2, 0, 1)
 SCATTER_ORDER = (1, 2, 0)
+FORWARD_GROUPS = ((0,), (1,), (2,))
+BACKWARD_GROUPS = ((1,), (2, 0))
 COPIES = 192
 CODED = 22
 GREETED = ("z+", "z-", "zz+", "zz-", "yh", "x+", "x-", "yl", "core")
@@ -76,6 +78,16 @@
     return sheet, padded.reshape(GX, 2 * FOLD)[xs]
 
 
+def group_rows(group):
+    return sum(SLOTS * SLAB_ROWS[k] for k in group)
+
+
+def spot_of(groups, k):
+    for g, group in enumerate(groups):
+        if k in group:
+            return g, group_rows(group[: group.index(k)]), group_rows(group)
+
+
 def split(x):
     high = x.astype(BF16)
     return high, (x - high.astype(F32)).astype(BF16)
@@ -165,7 +177,7 @@
 
 
 RATES = {"z": 1 / 49e3, "x": 1 / 49e3, "y": 1 / 49e3, "l": 1 / 49e3, "c": 1 / 400e3}
-DELAYS = {"z": 2.9, "x": 2.9, "y": 3.2, "l": 2.9, "c": 0.7}
+DELAYS = {'z': 3.6, 'x': 3.2, 'y': 3.8, 'l': 3.2, 'c': 0.8}
 
 
 class Task:
@@ -376,13 +388,12 @@
 def exchange_kernel(
     own_in, pair_list_in, pair_count_in, sheet_in, kernel_in, out,
     own, pair_list, pair_count, own_0, own_1, own_2, cols_0, cols_1, cols_2, rows_0, rows_1, rows_2,
-    dens_0, dens_1, dens_2, spec_0, spec_1, spec_2, first_0, first_1, first_2,
+    dens, spec, first_0, first_1, first_2,
     second_0, second_1, second_2, coded_0, coded_1, coded_2, codes_in_0, codes_in_1, codes_in_2,
     swapped_0, swapped_1, swapped_2, swaps_in_0, swaps_in_1, swaps_in_2,
     kept_0, kept_1, kept_2, sheet, kernel, send_sem, recv_sem, local_sem,
 ):
     owns, cols, rows = (own_0, own_1, own_2), (cols_0, cols_1, cols_2), (rows_0, rows_1, rows_2)
-    dens, spec = (dens_0, dens_1, dens_2), (spec_0, spec_1, spec_2)
     first_sums, second_sums = (first_0, first_1, first_2), (second_0, second_1, second_2)
     coded, codes_in = (coded_0, coded_1, coded_2), (codes_in_0, codes_in_1, codes_in_2)
     kept = (kept_0, kept_1, kept_2)
@@ -448,13 +459,14 @@
     def fill(k, slots):
         size = SLAB_ROWS[k]
         group = 16 // size
+        g, base, total = spot_of(FORWARD_GROUPS, k)
         for p in range(slots[0], slots[1], group):
             parts = [fold(density(k, p + i), k) for i in range(group)]
             for parity in range(2):
                 value = jnp.concatenate([part[parity] for part in parts], axis=0)
                 high, low = split(value)
-                dens[k][parity, pl.ds(p * size, 16), :] = high
-                dens[k][parity, pl.ds((SLOTS + p) * size, 16), :] = low
+                dens[g][parity, pl.ds(base + p * size, 16), :] = high
+                dens[g][parity, pl.ds(total + base + p * size, 16), :] = low
 
     def product(values, parity, at, width):
         lanes = pl.ds(at, width)
@@ -463,12 +475,14 @@
         thin = jnp.dot(values[:half], sheet[pl.ds((2 + parity) * FOLD, FOLD), lanes], preferred_element_type=F32)
         return wide[:half] + wide[half:] + thin
 
-    def forward(k, parity, at, width):
-        size = SLOTS * SLAB_ROWS[k]
-        high, low = split(product(dens[k][parity], parity, at, width))
+    def forward(g, parity, at, width):
+        high, low = split(product(dens[g][parity], parity, at, width))
         lanes = pl.ds(parity * FOLD + at, width)
-        spec[k][pl.ds(0, size), lanes] = high
-        spec[k][pl.ds(size, size), lanes] = low
+        for k in FORWARD_GROUPS[g]:
+            start, size = spot_of(FORWARD_GROUPS, k)[1], SLOTS * SLAB_ROWS[k]
+            b, base, total = spot_of(BACKWARD_GROUPS, k)
+            spec[b][pl.ds(base, size), lanes] = high[start : start + size]
+            spec[b][pl.ds(total + base, size), lanes] = low[start : start + size]
 
     def along():
         return sheet[pl.ds(4 * FOLD, 80), pl.ds(0, 240)]
@@ -481,8 +495,13 @@
         lanes = pl.ds(j * 256, 256)
         table = kernel[:, lanes]
         for q in range(SLOTS // 2):
+            def place_of(k, shift):
+                b, base, total = spot_of(BACKWARD_GROUPS, k)
+                return b, pl.ds(base + shift * total + 2 * q * SLAB_ROWS[k], 2 * SLAB_ROWS[k])
+
             def rows_of(shift):
-                return [spec[k][pl.ds((shift * SLOTS + 2 * q) * SLAB_ROWS[k], 2 * SLAB_ROWS[k]), lanes] for k in SLABS]
+                spots = [place_of(k, shift) for k in SLABS]
+                return [spec[b][some, lanes] for b, some in spots]
 
             high, low = rows_of(0), rows_of(1)
             turned = jnp.dot(along(), jnp.concatenate(high + low + high, axis=0), preferred_element_type=F32)
@@ -490,20 +509,25 @@
             at = 0
             for k in SLABS:
                 size = 2 * SLAB_ROWS[k]
-                spec[k][pl.ds(q * size, size), lanes] = high[at : at + size]
-                spec[k][pl.ds(SLOTS * SLAB_ROWS[k] + q * size, size), lanes] = low[at : at + size]
+                for shift, part in enumerate((high, low)):
+                    b, some = place_of(k, shift)
+                    spec[b][some, lanes] = part[at : at + size]
                 at += size
 
-    def backward(k, at, width):
-        size = SLAB_ROWS[k]
-        even = product(spec[k][:, pl.ds(0, FOLD)], 0, at, width)
-        odd = product(spec[k][:, pl.ds(FOLD, FOLD)], 1, at, width)
+    def backward(b, at, width):
+        even = product(spec[b][:, pl.ds(0, FOLD)], 0, at, width)
+        odd = product(spec[b][:, pl.ds(FOLD, FOLD)], 1, at, width)
         near, far = even + odd, even - odd
         if at == MAIN:
             lane = lax.broadcasted_iota(jnp.int32, near.shape, 1)
             near = jnp.where(lane < TAIL, near, pltpu.roll(far, TAIL, 1))
+        for k in BACKWARD_GROUPS[b]:
+            add_terms(k, near, far, spot_of(BACKWARD_GROUPS, k)[1], at, width)
+
+    def add_terms(k, near, far, base, at, width):
+        size = SLAB_ROWS[k]
         for p in range(SLOTS):
-            mine = slice(p * size, (p + 1) * size)
+            mine = slice(base + p * size, base + (p + 1) * size)
             if at == MAIN:
                 spans = [(WIDE - 128 if size == 16 else MAIN, near[mine])]
                 if size < 16:
@@ -567,24 +591,29 @@
         weight = SLAB_LANES[k] / WIDE
         for half in range(2):
             piece(f"fill{k}{half}", [*filled[k], "clear"], 0.25 * weight, functools.partial(fill, k, (4 * half, 4 * half + 4)))
+    for g, group in enumerate(FORWARD_GROUPS):
+        ready = [f"fill{k}{half}" for k in group for half in range(2)]
         for parity in range(2):
             for at, width in ((0, 512), (512, 384)):
-                name = f"forward{k}{parity}{at}"
+                name = f"forward{g}{parity}{at}"
                 turned.append(name)
-                piece(name, [f"fill{k}0", f"fill{k}1"], 0.3 * weight, functools.partial(forward, k, parity, at, width))
+                cost = 0.12 + 0.18 * group_rows(group) / 128
+                piece(name, ready, cost, functools.partial(forward, g, parity, at, width))
+
     def all_middle():
         for j in range(2 * FOLD // 256):
             middle(j)
 
     piece("middle", turned, 2.5, all_middle)
+    for b, group in enumerate(BACKWARD_GROUPS):
+        names = []
+        for at, width in ((0, 256), (256, 256), (512, 256), (768, 128)):
+            names.append(f"backward of {b}{at}")
+            cost = width / 256 * (0.3 + 0.3 * group_rows(group) / 128)
+            piece(names[-1], ["middle"], cost, functools.partial(backward, b, at, width))
+        for k in group:
+            tasks.append(Task(f"backward{k}", names, 0.0, nothing))
     for k in SCATTER_ORDER:
-        weight = SLAB_LANES[k] / WIDE
-        before, names = ["middle"], []
-        for at, width in ((0, 256), (256, 256), (512, 256), (768, 128)):
-            names.append(f"backward{k}{at}")
-            piece(names[-1], before, width / 256 * 0.6 * weight, functools.partial(backward, k, at, width))
-        piece(f"backward{k}", names, 0.0, nothing)
-        tasks[-1].rank = 0
         tasks += scatter_tasks(
             wires, place, k, functools.partial(last_slot, first_band), functools.partial(last_slot, second_band),
             first_sums[k], second_sums[k], coded[k], codes_in[k], swapped[k], swaps_in[k],
@@ -622,8 +651,8 @@
             *each(lambda k: (16, SLAB_LANES[k]), BF16),
             *each(stack(BANDS), BF16),
             *each(stack(BANDS), BF16),
-            *each(lambda k: (2, 2 * SLOTS * SLAB_ROWS[k], FOLD), BF16),
-            *each(lambda k: (2 * SLOTS * SLAB_ROWS[k], 2 * FOLD), BF16),
+            [pltpu.VMEM((2, 2 * group_rows(group), FOLD), BF16) for group in FORWARD_GROUPS],
+            [pltpu.VMEM((2 * group_rows(group), 2 * FOLD), BF16) for group in BACKWARD_GROUPS],
             *each(stack(SLOTS + 1), F32),
             *each(stack(SLOTS + 1), F32),
             *each(stack(CODED), I16),

time: 68.6 us -> 68.5 us (level); the launches traced: 68.4 us -> 67.2 us
  Pallas kernels: 65.8 us -> 64.6 us
    pallas_call x1, Pallas kernels: 65.8 us -> 64.6 us  [exchange(): pl.pallas_call(exchange_kernel, out_shape=jax.ShapeDtypeStruct((GX, GX *...]
where the time goes in v6:
time: 68.5 us; the launch traced here: 67.2 us
  Pallas kernels  64.6 us (94%)
  local copies, waits for them, and re-layouts  1.94 us (3%)
    pallas_call x1, Pallas kernels, exchange(): pl.pallas_call(exchange_kernel, out_shape=jax.ShapeDtypeStruct((GX, GX *...  64.6 us
    reshape x1, local copies, waits for them, and re-layouts, shards(): return fields.reshape(1, GX * GX * GX)  1.94 us

profile of v6, /device:TPU:8, one launch (start us, length us, event | category | flops | bytes accessed | tf_op | source)
XLA Modules:
  0.0 67.2 jit_solution(8335470938592557993)
XLA Ops:
  0.7 64.6 %exchange.1 = f32[40,1600]{1,0:T(8,128)} custom-call(bf16[1,64000]{1,0:T(2,128)(2,1)} %own_in.1, s32[1,2,8]{2,1,0:T(2,128)} %bitcast.1, s32[1]{0:T(128)S(6)} %copy.6.pair_count_in, bf16[3664,896]{1,0:T(8,128)(2,1)} %constant.4.clone.sheet_in, f32[80,1792]{1,0:T(8,128)} %constant.5.clone.kernel_in), custom_call_target="tpu_custom_call" | custom-call | tf_op jit(solution)/shard_map/exchange/pallas_call | solution.py:642
  65.2 1.9 %reshape.3 = f32[1,64000]{1,0:T(1,128)} reshape(f32[40,1600]{1,0:T(8,128)} %exchange.1) | data formatting | bytes 512000 | tf_op jit(solution)/shard_map/reshape | solution.py:678
